TPU v7x, 32 devices: a whole 2x2x4 slice. The times are simulated.
32 devices in a mesh: grp: 2 (over core), dp: 16 (over z, y, x).
Axes of the slice: x: 2, y: 2, z: 4, core: 2. Of those that a mesh axis runs over, the one named last changes fastest.
Arguments:
- tokens: bfloat16 [32768, 768], P(('grp', 'dp')), may hold values from -6 to 6
- out_grad: bfloat16 [32768, 768], P(('grp', 'dp')), may hold values from -6 to 6
- image_counts: int32 [32, 32], P(('grp', 'dp')), may hold values from 0 to 98, as said below
- group_of_device: int32 [32], P(('grp', 'dp')), may hold values from 0 to 2, as said below
- group_weight: int32 [3], replicated, may hold values from 1 to 4
- norm1_gain: bfloat16 [768], replicated, may hold values from 0.5 to 1.5
- norm1_bias: bfloat16 [768], replicated, may hold values from -4 to 4
- qkv_weight: bfloat16 [768, 2304], replicated, may hold values from -0.21875 to 0.21875
- qkv_bias: bfloat16 [2304], replicated, may hold values from -4 to 4
- proj_weight: bfloat16 [768, 768], replicated, may hold values from -0.875 to 0.875
- proj_bias: bfloat16 [768], replicated, may hold values from -4 to 4
- norm2_gain: bfloat16 [768], replicated, may hold values from 0.5 to 1.5
- norm2_bias: bfloat16 [768], replicated, may hold values from -4 to 4
- fc1_weight: bfloat16 [768, 3072], replicated, may hold values from -0.21875 to 0.21875
- fc1_bias: bfloat16 [3072], replicated, may hold values from -4 to 4
- fc2_weight: bfloat16 [3072, 768], replicated, may hold values from -0.109375 to 0.109375
- fc2_bias: bfloat16 [768], replicated, may hold values from -4 to 4
- first_moment: float32 [16, 442992], P('dp'), may hold values from -2.5 to 2.5
- second_moment: float32 [16, 442992], P('dp'), may hold values from 1e-05 to 0.001
Outputs:
- block_out: bfloat16 [32768, 768], P(('grp', 'dp'))
- input_grad: bfloat16 [32768, 768], P(('grp', 'dp'))
- weight_grads: float32 [16, 442992], P('dp')
- new_weights: bfloat16 [16, 442992], replicated
- new_first: float32 [16, 442992], P('dp')
- new_second: float32 [16, 442992], P('dp')
- fc2_bias_grad: float32 [768], P('dp')
Inputs may be any that keep to these rules, and one draw needn't show every extreme that they name: `group_of_device`: each of the 3 groups holds some devices: about a half, a third and a sixth of them. `image_counts`: in each device's row the live images come first, at least one, each with 30 to 98 visible patches, summing to at most 1024; the remaining slots are 0.
All inputs are finite; a program needn't handle non-finite values.
Results may differ from a plain program's by a relative error of at most 0.012.
Values may be sent and summed in bfloat16 or wider, within the bound.
No kernel may reach another device: no remote copies, remote signals or barrier semaphores. Data moves between devices by JAX's collectives and lax.ppermute only.
A program may use at most 320 MiB of HBM per device.

v0:
```python
import jax
import jax.numpy as jnp
from jax import lax
from jax.sharding import PartitionSpec as P

D = 768
HEADS = 12
HEAD_DIM = 64
NGROUPS = 3


beta_one = 0.9
beta_two = 0.999
adam_eps = 1e-08
decay_rate = 0.05
step_count = 10.0
learn_rate = 0.004 * 0.75**1
norm_eps = 1e-06
neg_fill = -1e30
decay_flags = (0.0, 0.0, 1.0, 0.0, 1.0, 0.0, 0.0, 0.0, 1.0, 0.0, 1.0, 0.0)


def layer_norm(values, gain, shift):
    center = values - jnp.mean(values, axis=-1, keepdims=True)
    spread = jnp.mean(center * center, axis=-1, keepdims=True)
    return center * lax.rsqrt(spread + norm_eps) * gain + shift


def gelu_tanh(values):
    return jax.nn.gelu(values, approximate=True)


def contract_rows(first_op, second_op):
    return lax.dot_general(
        first_op, second_op, (((0,), (0,)), ((), ())), preferred_element_type=jnp.float32
    )


def contract_cols(first_op, second_op):
    return lax.dot_general(
        first_op, second_op, (((1,), (1,)), ((), ())), preferred_element_type=jnp.float32
    )


def segment_info(counts_row, length):
    segment_ends = jnp.cumsum(counts_row)
    position = lax.iota(jnp.int32, length)
    segment = jnp.sum((position[:, None] >= segment_ends[None, :]).astype(jnp.int32), axis=1)
    return (segment, position < segment_ends[-1])


def score_block(query_part, key_rows, same_segment):
    raw = (
        jnp.einsum("qhd,khd->hqk", query_part, key_rows, preferred_element_type=jnp.float32) * 0.125
    )
    return jnp.where(same_segment[None], raw, neg_fill)


def on_device(
    tokens,
    out_grad,
    image_counts,
    group_of_device,
    group_weight,
    norm1_gain,
    norm1_bias,
    qkv_weight,
    qkv_bias,
    proj_weight,
    proj_bias,
    norm2_gain,
    norm2_bias,
    fc1_weight,
    fc1_bias,
    fc2_weight,
    fc2_bias,
    first_moment,
    second_moment,
):
    length = tokens.shape[0]
    segment, valid_rows = segment_info(image_counts[0], length)
    images = jnp.sum((image_counts[0] > 0).astype(jnp.int32))
    member = (group_of_device[0] == lax.iota(jnp.int32, NGROUPS)).astype(jnp.int32)
    totals = lax.psum(member * images, ("grp", "dp"))
    factor = jnp.sum(member * group_weight).astype(jnp.float32) / jnp.sum(member * totals).astype(
        jnp.float32
    )
    inputs = tokens.astype(jnp.float32)
    normed_one, norm_one_back = jax.vjp(
        layer_norm, inputs, norm1_gain.astype(jnp.float32), norm1_bias.astype(jnp.float32)
    )
    normed_one_low = normed_one.astype(jnp.bfloat16)
    projected = (
        jnp.dot(normed_one_low, qkv_weight, preferred_element_type=jnp.float32)
        + qkv_bias.astype(jnp.float32)
    ).astype(jnp.bfloat16)
    query_rows = projected[:, :D].reshape(length, HEADS, HEAD_DIM)
    key_rows = projected[:, D : 2 * D].reshape(length, HEADS, HEAD_DIM)
    value_rows = projected[:, 2 * D :].reshape(length, HEADS, HEAD_DIM)
    block_rows = min(512, length)
    offsets = list(range(0, length, block_rows))
    context_parts = []
    log_sums = []
    for offset in offsets:
        same_segment = segment[offset : offset + block_rows, None] == segment[None, :]
        scores = score_block(query_rows[offset : offset + block_rows], key_rows, same_segment)
        row_max = jnp.max(scores, axis=-1, keepdims=True)
        exponent = jnp.exp(scores - row_max)
        row_sum = jnp.sum(exponent, axis=-1, keepdims=True)
        attn_probs = exponent / row_sum
        log_sums.append(row_max + jnp.log(row_sum))
        context_parts.append(
            jnp.einsum(
                "hqk,khd->qhd",
                attn_probs.astype(jnp.bfloat16),
                value_rows,
                preferred_element_type=jnp.float32,
            )
        )
    context = jnp.concatenate(context_parts, axis=0).reshape(length, D).astype(jnp.bfloat16)
    middle = inputs + (
        jnp.dot(context, proj_weight, preferred_element_type=jnp.float32)
        + proj_bias.astype(jnp.float32)
    )
    normed_two, norm_two_back = jax.vjp(
        layer_norm, middle, norm2_gain.astype(jnp.float32), norm2_bias.astype(jnp.float32)
    )
    normed_two_low = normed_two.astype(jnp.bfloat16)
    hidden = jnp.dot(
        normed_two_low, fc1_weight, preferred_element_type=jnp.float32
    ) + fc1_bias.astype(jnp.float32)
    activated, gelu_back = jax.vjp(gelu_tanh, hidden)
    activated_low = activated.astype(jnp.bfloat16)
    block_out = (
        middle
        + (
            jnp.dot(activated_low, fc2_weight, preferred_element_type=jnp.float32)
            + fc2_bias.astype(jnp.float32)
        )
    ).astype(jnp.bfloat16)
    grad_out = out_grad.astype(jnp.float32) * valid_rows[:, None].astype(jnp.float32)
    grad_out_low = grad_out.astype(jnp.bfloat16)
    fc2_grad = contract_rows(activated_low, grad_out_low)
    fc2_bias_grad = jnp.sum(grad_out, axis=0)
    grad_hidden = gelu_back(contract_cols(grad_out_low, fc2_weight))[0].astype(jnp.bfloat16)
    fc1_grad = contract_rows(normed_two_low, grad_hidden)
    fc1_bias_grad = jnp.sum(grad_hidden.astype(jnp.float32), axis=0)
    grad_middle_norm, gain_two_grad, shift_two_grad = norm_two_back(
        contract_cols(grad_hidden, fc1_weight)
    )
    grad_middle = grad_out + grad_middle_norm
    grad_branch = grad_middle.astype(jnp.bfloat16)
    proj_grad = contract_rows(context, grad_branch)
    proj_bias_grad = jnp.sum(grad_branch.astype(jnp.float32), axis=0)
    grad_context = (
        contract_cols(grad_branch, proj_weight)
        .astype(jnp.bfloat16)
        .reshape(length, HEADS, HEAD_DIM)
    )
    grad_keys = jnp.zeros((length, HEADS, HEAD_DIM), jnp.float32)
    grad_values = jnp.zeros((length, HEADS, HEAD_DIM), jnp.float32)
    query_grads = []
    for piece_index, offset in enumerate(offsets):
        query_part = query_rows[offset : offset + block_rows]
        context_grad_part = grad_context[offset : offset + block_rows]
        same_segment = segment[offset : offset + block_rows, None] == segment[None, :]
        attn_probs = jnp.exp(
            score_block(query_part, key_rows, same_segment) - log_sums[piece_index]
        )
        grad_probs = jnp.einsum(
            "qhd,khd->hqk", context_grad_part, value_rows, preferred_element_type=jnp.float32
        )
        grad_scores = (
            attn_probs * (grad_probs - jnp.sum(attn_probs * grad_probs, axis=-1, keepdims=True))
        ).astype(jnp.bfloat16)
        query_grads.append(
            jnp.einsum("hqk,khd->qhd", grad_scores, key_rows, preferred_element_type=jnp.float32)
            * 0.125
        )
        grad_keys = (
            grad_keys
            + jnp.einsum(
                "hqk,qhd->khd", grad_scores, query_part, preferred_element_type=jnp.float32
            )
            * 0.125
        )
        grad_values = grad_values + jnp.einsum(
            "hqk,qhd->khd",
            attn_probs.astype(jnp.bfloat16),
            context_grad_part,
            preferred_element_type=jnp.float32,
        )
    grad_projected = jnp.concatenate(
        [
            jnp.concatenate(query_grads, axis=0).reshape(length, D),
            grad_keys.reshape(length, D),
            grad_values.reshape(length, D),
        ],
        axis=1,
    ).astype(jnp.bfloat16)
    qkv_grad = contract_rows(normed_one_low, grad_projected)
    qkv_bias_grad = jnp.sum(grad_projected.astype(jnp.float32), axis=0)
    grad_input_norm, gain_one_grad, shift_one_grad = norm_one_back(
        contract_cols(grad_projected, qkv_weight)
    )
    input_grad = (grad_middle + grad_input_norm).astype(jnp.bfloat16)
    row_count = lax.axis_size("dp")
    grad_list = (
        gain_one_grad,
        shift_one_grad,
        qkv_grad,
        qkv_bias_grad,
        proj_grad,
        proj_bias_grad,
        gain_two_grad,
        shift_two_grad,
        fc1_grad,
        fc1_bias_grad,
        fc2_grad,
        fc2_bias_grad,
    )
    packed = jnp.concatenate(
        [(grad_item * factor).reshape(row_count, -1) for grad_item in grad_list], axis=1
    )
    grad_part = lax.psum_scatter(packed, "dp", scatter_dimension=0, tiled=True)
    summed = lax.psum(grad_part, "grp")
    bias_width = fc2_bias.shape[0] // row_count
    summed_bias = summed[0, summed.shape[1] - bias_width :]
    own_index = lax.axis_index("dp")
    weight_list = (
        norm1_gain,
        norm1_bias,
        qkv_weight,
        qkv_bias,
        proj_weight,
        proj_bias,
        norm2_gain,
        norm2_bias,
        fc1_weight,
        fc1_bias,
        fc2_weight,
        fc2_bias,
    )
    current = jnp.concatenate(
        [
            lax.dynamic_slice_in_dim(weight_item.reshape(row_count, -1), own_index, 1, 0).astype(
                jnp.float32
            )
            for weight_item in weight_list
        ],
        axis=1,
    )
    decay = jnp.concatenate(
        [
            jnp.full((1, weight_item.size // row_count), decay_flag, jnp.float32)
            for weight_item, decay_flag in zip(weight_list, decay_flags)
        ],
        axis=1,
    )
    new_first = beta_one * first_moment + (1.0 - beta_one) * summed
    new_second = beta_two * second_moment + (1.0 - beta_two) * summed * summed
    ratio = (
        new_first
        / (1.0 - beta_one**step_count)
        / (jnp.sqrt(new_second / (1.0 - beta_two**step_count)) + adam_eps)
    )
    fresh_low = (current - learn_rate * (ratio + decay_rate * decay * current)).astype(jnp.bfloat16)
    new_weights = lax.all_gather(fresh_low, "dp", axis=0, tiled=True)
    return (block_out, input_grad, summed, new_weights, new_first, new_second, summed_bias)


def solution(mesh):
    in_specs = (
        P(("grp", "dp"), None),
        P(("grp", "dp"), None),
        P(("grp", "dp"), None),
        P(("grp", "dp")),
        P(),
        P(),
        P(),
        P(),
        P(),
        P(),
        P(),
        P(),
        P(),
        P(),
        P(),
        P(),
        P(),
        P("dp", None),
        P("dp", None),
    )
    out_specs = (
        P(("grp", "dp"), None),
        P(("grp", "dp"), None),
        P("dp", None),
        P(),
        P("dp", None),
        P("dp", None),
        P("dp"),
    )
    return jax.shard_map(
        on_device, mesh=mesh, in_specs=in_specs, out_specs=out_specs, check_vma=False
    )
```

profile of v0, /device:TPU:0, one launch (start us, length us, event | category | flops | bytes accessed | tf_op | source)
XLA Modules:
  0.0 1624.4 jit_solution(11156478044281256966)
XLA Ops:
  26.9 12.2 fusion.19
  39.1 11.8 fusion
  54.0 12.7 fusion.44
  69.0 12.2 fusion.20
  81.2 13.4 fusion.1
  97.1 8.5 fusion.45
  114.4 10.8 fusion.63
  125.3 16.5 %convert_reduce_fusion = (f32[3072]{0:T(1024)}, bf16[1024,3072]{1,0:T(8,128)(2,1)S(1)}) fusion(f32[1024,3072]{1,0:T(8,128)} %fusion.63, f32[3072]{0:T(1024)S(1)} %convert_element_type.143, bf16[3072,768]{1,0:T(8,128)(2,1)} %param.34, bf16[1024,768]{0,1:T(8,128)(2,1)S(1)} %copy-done.14, f32[1024]{0:T(1024)S(1)} %fusion.47), kind=kOutput, calls=%fused_computation.28 | convolution fusion | flops 4906546176 | bytes 25194496 | tf_op jit(solution)/shard_map/dot_general | solution.py:40
  162.6 21.8 %multiply_reduce_fusion.1 = (f32[12,512]{1,0:T(8,128)S(1)}, f32[12,512,1024]{2,1,0:T(8,128)}) fusion(f32[12,512]{1,0:T(8,128)S(1)} %copy-done.43, f32[12,512,1024]{2,1,0:T(8,128)} %get-tuple-element.68, pred[512,1024]{1,0:T(8,128)(4,1)S(1)} %copy-done.18, bf16[512,12,64]{0,2,1:T(8,128)(2,1)S(1)} %bitcast.95, bf16[1024,12,64]{0,2,1:T(8,128)(2,1)S(1)} %bitcast.81), kind=kOutput, calls=%fused_computation.4 | convolution fusion | flops 836757504 | bytes 53264384 | tf_op jit(solution)/shard_map/qhd,khd->hqk/dot_general | solution.py:170
  184.5 17.7 %multiply_reduce_fusion = (f32[12,512]{1,0:T(8,128)S(1)}, f32[12,512,1024]{2,1,0:T(8,128)}) fusion(f32[12,512]{1,0:T(8,128)S(1)} %log_add_fusion, f32[12,512,1024]{2,1,0:T(8,128)} %get-tuple-element.66, pred[512,1024]{1,0:T(8,128)(4,1)S(1)} %copy-done.20, bf16[512,12,64]{0,2,1:T(8,128)(2,1)} %bitcast.97, bf16[1024,12,64]{0,2,1:T(8,128)(2,1)S(1)} %bitcast.82), kind=kOutput, calls=%fused_computation.1 | convolution fusion | flops 836757504 | bytes 53264384 | tf_op jit(solution)/shard_map/qhd,khd->hqk/dot_general | solution.py:170
  202.2 42.0 %multiply_convert_fusion = (bf16[12,512,1024]{2,1,0:T(8,128)(2,1)}, bf16[12,512,1024]{2,1,0:T(8,128)(2,1)}) fusion(f32[12,512,1024]{2,1,0:T(8,128)} %get-tuple-element.74, f32[12,512]{1,0:T(8,128)S(1)} %get-tuple-element.73, f32[12,512]{1,0:T(8,128)S(1)} %log_add_fusion, f32[12,512,1024]{2,1,0:T(8,128)} %get-tuple-element.66, ...), kind=kLoop, calls=%fused_computation | loop fusion | flops 75497472 | bytes 126976000 | tf_op jit(solution)/shard_map/convert_element_type | solution.py:175
  244.1 9.6 fusion.42
  253.8 8.8 fusion.74
  262.5 13.4 fusion.11
  288.4 13.0 add_convert_fusion.2
  311.9 42.4 %psum.14 = s32[3]{0:T(128)S(1)} all-reduce(s32[3]{0:T(128)S(1)} %fusion.51), channel_id=1, replica_groups=mesh['grp'=2,'dp'=16] {'grp','dp'}, use_global_device_ids=true, to_apply=%region_19.20 | all-reduce | flops 3 | bytes 24 | tf_op jit(solution)/shard_map/psum | solution.py:84
  357.0 9.0 convolution_multiply_fusion
  369.0 10.7 convolution_multiply_fusion.2
  379.8 10.9 convolution_multiply_fusion.1
  407.6 10.7 reshape.520
  418.4 10.6 reshape.521
  437.5 20.7 %dynamic-update-slice.24 = f32[16,442992]{1,0:T(8,128)} dynamic-update-slice(f32[16,442992]{1,0:T(8,128)} %dynamic-update-slice.23, f32[16,110592]{1,0:T(8,128)} %reshape.518, s32[]{} %constant.87, s32[]{} %constant.88) | dynamic-update-slice | bytes 14155780
  479.6 27.0 %dynamic-update-slice.32 = f32[16,442992]{1,0:T(8,128)} dynamic-update-slice(f32[16,442992]{1,0:T(8,128)} %dynamic-update-slice.31, f32[16,147456]{1,0:T(8,128)} %reshape.521, s32[]{} %constant.87, s32[]{} %constant.95) | dynamic-update-slice | bytes 18874372
  533.6 8.7 dynamic-update-slice.1
  554.9 8.8 dynamic-update-slice.12
  576.0 667.0 %all-reduce.6.cloned.1.call-done = f32[16,442992]{1,0:T(8,128)} async-done(((f32[16,442992]{1,0:T(8,128)}), f32[16,442992]{1,0:T(8,128)}) %all-reduce.6.cloned.1.call-update) | async-done | bytes 28351504
  1255.5 11.4 dynamic-update-slice.8
  1269.4 11.3 dynamic-update-slice.20
  1282.0 14.6 convert_bitcast_fusion
  1299.4 11.8 add_convert_fusion.3
  1315.0 282.6 %all-gather.3.cloned.1.call-done = bf16[16,1,442992]{2,1,0:T(2,128)(2,1)} async-done(((bf16[1,1,442992]{2,1,0:T(2,128)(2,1)}), bf16[16,1,442992]{2,1,0:T(2,128)(2,1)}) %all-gather.3.cloned.1.call-update) | async-done | bytes 14175760 | tf_op jit(solution)/shard_map/all_gather | solution.py:268
  1597.7 18.5 %copy.107 = bf16[16,1,442992]{2,0,1:T(8,128)(2,1)} copy(bf16[16,1,442992]{2,1,0:T(2,128)(2,1)} %all-gather.3.cloned.1.call-done) | data formatting | bytes 28351488
  (329 shorter events, 206.0 us)
Async XLA Ops:
  7.2 1235.7 %all-reduce.6.cloned.1.call-start = ((), (), s32[]{:S(2)}) async-start(), calls=%async_computation.2 | async-start | bytes 56705024
  9.0 98.1 %copy-start.1 = (bf16[1024,768]{0,1:T(8,128)(2,1)}, bf16[1024,768]{0,1:T(8,128)(2,1)S(1)}, u32[]{:S(2)}) copy-start(bf16[1024,768]{0,1:T(8,128)(2,1)S(1)} %copy.90) | copy-start | bytes 4718596
  22.5 46.6 %copy-start.8 = (bf16[1024,768]{0,1:T(8,128)(2,1)}, bf16[1024,768]{0,1:T(8,128)(2,1)S(1)}, u32[]{:S(2)}) copy-start(bf16[1024,768]{0,1:T(8,128)(2,1)S(1)} %copy.94) | copy-start | bytes 4718596
  26.9 12.2 copy-start.17
  69.0 25.7 %copy-start.12 = (bf16[1024,768]{0,1:T(8,128)(2,1)S(1)}, bf16[1024,768]{0,1:T(8,128)(2,1)}, u32[]{:S(2)}) copy-start(bf16[1024,768]{0,1:T(8,128)(2,1)} %copy.91) | copy-start | bytes 4718596
  81.2 15.8 copy-start
  81.2 15.9 copy-start.19
  110.9 14.4 copy-start.41
  114.4 10.9 copy-start.60
  114.4 27.3 %slice-start.3 = ((s8[4718592]{0:T(1024)(128)(4,1)}), s8[4194304]{0:T(1024)(128)(4,1)S(1)}, s32[]{:S(2)}) async-start(s8[4718592]{0:T(1024)(128)(4,1)} %bitcast.76), calls=%async_computation.6 | async-start | bytes 8388608
  125.3 16.5 %slice-start.4 = ((s8[4718592]{0:T(1024)(128)(4,1)}), s8[524288]{0:T(1024)(128)(4,1)S(1)}, s32[]{:S(2)}) async-start(s8[4718592]{0:T(1024)(128)(4,1)} %bitcast.76), calls=%async_computation.7 | async-start | bytes 1048576
  161.8 22.6 %copy-start.30 = (bf16[512,768]{0,1:T(8,128)(2,1)}, bf16[512,768]{0,1:T(8,128)(2,1)S(1)}, u32[]{:S(2)}) copy-start(bf16[512,768]{0,1:T(8,128)(2,1)S(1)} %get-tuple-element.59) | copy-start | bytes 2359300
  162.6 21.9 %copy-start.20 = (pred[512,1024]{1,0:T(8,128)(4,1)S(1)}, pred[512,1024]{1,0:T(8,128)(4,1)}, u32[]{:S(2)}) copy-start(pred[512,1024]{1,0:T(8,128)(4,1)} %get-tuple-element.62) | copy-start | bytes 1572868
  202.2 42.0 %copy-start.9 = (bf16[1024,768]{0,1:T(8,128)(2,1)S(1)}, bf16[1024,768]{0,1:T(8,128)(2,1)}, u32[]{:S(2)}) copy-start(bf16[1024,768]{0,1:T(8,128)(2,1)} %copy-done.8) | copy-start | bytes 4718596
  253.7 22.8 %slice-start = ((s8[12582912]{0:T(1024)(128)(4,1)}), s8[4194304]{0:T(1024)(128)(4,1)S(1)}, s32[]{:S(2)}) async-start(s8[12582912]{0:T(1024)(128)(4,1)} %bitcast.70), calls=%async_computation.3 | async-start | bytes 8388608
  253.7 22.8 %slice-start.1 = ((s8[12582912]{0:T(1024)(128)(4,1)}), s8[4194304]{0:T(1024)(128)(4,1)S(1)}, s32[]{:S(2)}) async-start(s8[12582912]{0:T(1024)(128)(4,1)} %bitcast.70), calls=%async_computation.4 | async-start | bytes 8388608
  262.5 13.4 copy-start.77
  262.5 14.0 slice-start.2
  288.4 13.1 copy-start.28
  288.4 13.1 copy-start.29
  305.1 50.5 %copy-start.78 = (s32[3]{0:T(128)S(1)}, s32[3]{0:T(128)}, u32[]{:S(2)}) copy-start(s32[3]{0:T(128)} %param.23) | copy-start | bytes 40
  305.1 51.9 %copy-start.2 = (bf16[1024,768]{0,1:T(8,128)(2,1)S(1)}, bf16[1024,768]{0,1:T(8,128)(2,1)}, u32[]{:S(2)}) copy-start(bf16[1024,768]{0,1:T(8,128)(2,1)} %copy-done.1) | copy-start | bytes 4718596
  305.1 51.9 %copy-start.45 = (f32[1024]{0:T(1024)S(1)}, f32[1024]{0:T(1024)}, u32[]{:S(2)}) copy-start(f32[1024]{0:T(1024)} %copy-done.44) | copy-start | bytes 12292
  305.1 51.9 %copy-start.47 = (f32[768]{0:T(1024)S(1)}, f32[768]{0:T(1024)}, u32[]{:S(2)}) copy-start(f32[768]{0:T(1024)} %copy-done.46) | copy-start | bytes 9220
  305.1 51.9 %copy-start.49 = (f32[1024]{0:T(1024)S(1)}, f32[1024]{0:T(1024)}, u32[]{:S(2)}) copy-start(f32[1024]{0:T(1024)} %copy-done.48) | copy-start | bytes 12292
  305.1 51.9 %copy-start.74 = (f32[768]{0:T(1024)S(1)}, f32[768]{0:T(1024)}, u32[]{:S(2)}) copy-start(f32[768]{0:T(1024)} %copy-done.73) | copy-start | bytes 9220
  366.1 13.7 slice-start.5
  437.5 22.2 %copy-start.23 = (f32[16,36864]{1,0:T(8,128)S(1)}, f32[16,36864]{1,0:T(8,128)}, u32[]{:S(2)}) copy-start(f32[16,36864]{1,0:T(8,128)} %reshape.519) | copy-start | bytes 7077892
  507.9 774.1 %all-reduce.4.cloned.1.call-start = ((), (), s32[]{:S(2)}) async-start(), calls=%async_computation | async-start | bytes 3544064 | tf_op jit(solution)/shard_map/psum | solution.py:226
  1250.5 31.5 %copy-start.32 = (f32[1,442992]{1,0:T(1,128)S(1)}, f32[1,442992]{1,0:T(1,128)}, u32[]{:S(2)}) copy-start(f32[1,442992]{1,0:T(1,128)} %param.36) | copy-start | bytes 5315908
  1250.5 347.2 %all-gather.3.cloned.1.call-start = ((), (), s32[]{:S(2)}) async-start(), calls=%async_computation.1 | async-start | bytes 30124544 | tf_op jit(solution)/shard_map/all_gather | solution.py:268
  1315.0 301.2 %copy-start.25 = (f32[1,442992]{1,0:T(1,128)S(1)}, f32[1,442992]{1,0:T(1,128)}, u32[]{:S(2)}) copy-start(f32[1,442992]{1,0:T(1,128)} %all-reduce.4.cloned.1.call-done) | copy-start | bytes 5315908
  (59 other events, 290.8 us)
Sparse Core Ops, SparseCore 0:
  508.1 734.8 all-reduce.5
  1250.6 19.8 all-reduce.3
  1296.8 300.8 all-gather.2
where the time goes:
time: 1640 us; the launch traced here: 1620 us
  waiting for transfers between devices  950 us (58%)
  local copies, waits for them, and re-layouts  272 us (17%)
  matrix products  237 us (14%)
  other arithmetic  106 us (6%)
  blocking collectives  42.4 us (3%)
  between operations  17.2 us (1%)
    unnamed x4, waiting for transfers between devices  667 us
    all_gather x1, waiting for transfers between devices, on_device(): new_weights = lax.all_gather(fresh_low, 'dp', axis=0, tiled=True)  283 us
    unnamed x215, local copies, waits for them, and re-layouts  188 us
    psum x1, blocking collectives, on_device(): totals = lax.psum(member * images, ('grp', 'dp'))  42.4 us
    convert_element_type x1, other arithmetic, on_device(): grad_scores = (attn_probs * (grad_probs - jnp.sum(attn_probs * grad_probs...  42 us
    dot_general x2, matrix products, on_device(): jnp.einsum('qhd,khd->hqk', context_grad_part, value_rows, preferred_eleme...  39.6 us
    dot_general x4, matrix products, contract_rows(): lax.dot_general(first_op, second_op, (((0,), (0,)), ((), ())), preferred_...  33.5 us
  transfers between devices with their start and end apart: 3, of which 2 were waited for; matrix products, arithmetic and copies ran while one was open for 7% of the time, Pallas kernels for 0%

commit v1 on v0

--- a/solution.py
+++ b/solution.py
@@ -43,7 +43,10 @@
 
 
 def segment_info(counts_row, length):
-    segment_ends = jnp.cumsum(counts_row)
+    slots = lax.iota(jnp.int32, counts_row.shape[0])
+    segment_ends = jnp.sum(
+        jnp.where(slots[:, None] <= slots[None, :], counts_row[:, None], 0), axis=0
+    )
     position = lax.iota(jnp.int32, length)
     segment = jnp.sum((position[:, None] >= segment_ends[None, :]).astype(jnp.int32), axis=1)
     return (segment, position < segment_ends[-1])
@@ -204,28 +207,13 @@
         contract_cols(grad_projected, qkv_weight)
     )
     input_grad = (grad_middle + grad_input_norm).astype(jnp.bfloat16)
+    moments = (first_moment, second_moment)
+    mlp_summed, rest_summed = exchange_grads(
+        (gain_one_grad, shift_one_grad, qkv_grad, qkv_bias_grad, proj_grad, proj_bias_grad),
+        (gain_two_grad, shift_two_grad, fc1_grad, fc1_bias_grad, fc2_grad, fc2_bias_grad),
+        factor,
+    )
     row_count = lax.axis_size("dp")
-    grad_list = (
-        gain_one_grad,
-        shift_one_grad,
-        qkv_grad,
-        qkv_bias_grad,
-        proj_grad,
-        proj_bias_grad,
-        gain_two_grad,
-        shift_two_grad,
-        fc1_grad,
-        fc1_bias_grad,
-        fc2_grad,
-        fc2_bias_grad,
-    )
-    packed = jnp.concatenate(
-        [(grad_item * factor).reshape(row_count, -1) for grad_item in grad_list], axis=1
-    )
-    grad_part = lax.psum_scatter(packed, "dp", scatter_dimension=0, tiled=True)
-    summed = lax.psum(grad_part, "grp")
-    bias_width = fc2_bias.shape[0] // row_count
-    summed_bias = summed[0, summed.shape[1] - bias_width :]
     own_index = lax.axis_index("dp")
     weight_list = (
         norm1_gain,
@@ -241,32 +229,182 @@
         fc2_weight,
         fc2_bias,
     )
-    current = jnp.concatenate(
+    own_weights = [
+        lax.dynamic_slice_in_dim(item.reshape(row_count, -1), own_index, 1, 0)[0]
+        for item in weight_list
+    ]
+    rows = D // row_count
+    fc1_sum = mlp_summed[0].reshape(4, rows, D).transpose(1, 0, 2).reshape(-1)
+    fc2_sum = mlp_summed[1].reshape(-1)
+    qkv_sum = jnp.concatenate(
+        [rest_summed[0, :rows], rest_summed[0, rows : 2 * rows], rest_summed[1, :rows]], axis=1
+    ).reshape(-1)
+    proj_sum = rest_summed[1, rows : 2 * rows].reshape(-1)
+    small = rest_summed[0, 2 * rows]
+    widths = [item.size // row_count for item in weight_list]
+    small_parts = {}
+    start = 0
+    for index, flag in enumerate(decay_flags):
+        if flag == 0.0:
+            small_parts[index] = small[start : start + widths[index]]
+            start += widths[index]
+    large_parts = {2: qkv_sum, 4: proj_sum, 8: fc1_sum, 10: fc2_sum}
+    pieces = [
+        small_parts[index] if index in small_parts else large_parts[index] for index in range(12)
+    ]
+    split = sum(widths[:8])
+    grads_out, first_out, second_out, fresh = [], [], [], []
+    for lead, tail, begin, end in ((8, 12, split, sum(widths)), (0, 8, 0, split)):
+        summed_part = jnp.concatenate(pieces[lead:tail])
+        current = jnp.concatenate(own_weights[lead:tail]).astype(jnp.float32)
+        decay = jnp.concatenate(
+            [
+                jnp.full((width,), flag, jnp.float32)
+                for width, flag in zip(widths[lead:tail], decay_flags[lead:tail])
+            ]
+        )
+        new_first = beta_one * moments[0][0, begin:end] + (1.0 - beta_one) * summed_part
+        new_second = (
+            beta_two * moments[1][0, begin:end] + (1.0 - beta_two) * summed_part * summed_part
+        )
+        ratio = (
+            new_first
+            / (1.0 - beta_one**step_count)
+            / (jnp.sqrt(new_second / (1.0 - beta_two**step_count)) + adam_eps)
+        )
+        fresh_low = (current - learn_rate * (ratio + decay_rate * decay * current)).astype(
+            jnp.bfloat16
+        )
+        grads_out.insert(0, summed_part)
+        first_out.insert(0, new_first)
+        second_out.insert(0, new_second)
+        fresh.insert(0, gather_rows(fresh_low))
+    summed = jnp.concatenate(grads_out)[None]
+    new_first = jnp.concatenate(first_out)[None]
+    new_second = jnp.concatenate(second_out)[None]
+    new_weights = jnp.concatenate(fresh, axis=1)
+    summed_bias = pieces[11]
+    return (block_out, input_grad, summed, new_weights, new_first, new_second, summed_bias)
+
+
+AXES = ("grp", "dp")
+
+
+def swap(values, bit):
+    count = lax.axis_size("grp") * lax.axis_size("dp")
+    return lax.ppermute(values, AXES, [(i, i ^ bit) for i in range(count)])
+
+
+def bit_of(position):
+    return (lax.axis_index("dp") >> position) & 1
+
+
+def add_low(kept, came):
+    return (kept.astype(jnp.float32) + came.astype(jnp.float32)).astype(jnp.bfloat16)
+
+
+def halve(values, position, positions):
+    axis = positions.index(position)
+    own = bit_of(position)
+    sent = lax.dynamic_index_in_dim(values, 1 - own, axis, keepdims=False)
+    kept = lax.dynamic_index_in_dim(values, own, axis, keepdims=False)
+    return kept, swap(sent, 1 << position), [p for p in positions if p != position]
+
+
+def reduce_rows(values):
+    count = lax.axis_size("dp")
+    grp = lax.axis_index("grp")
+    kept = lax.dynamic_index_in_dim(values, grp, 0, keepdims=False)
+    came = swap(lax.dynamic_index_in_dim(values, 1 - grp, 0, keepdims=False), count)
+    kept = add_low(kept, came)
+    depth = count.bit_length() - 1
+    positions = list(range(depth))[::-1]
+    rows = kept.shape[1]
+    parts = [kept[:, : rows // 2], kept[:, rows // 2 :]]
+    left = [positions, positions]
+    parts = [part.reshape((2,) * depth + part.shape[1:]) for part in parts]
+    for order in ((0, 1), (1, 0)):
+        for index in (0, 1):
+            part, came, left[index] = halve(parts[index], order[index], left[index])
+            parts[index] = add_low(part, came)
+    whole = jnp.concatenate(parts, axis=depth - 2)
+    rest = left[0]
+    for position in range(2, depth):
+        part, came, rest = halve(whole, position, rest)
+        if rest:
+            whole = add_low(part, came)
+        else:
+            whole = part.astype(jnp.float32) + came.astype(jnp.float32)
+    other = swap(whole, count)
+    return jnp.where(grp == 0, jnp.stack([whole, other]), jnp.stack([other, whole]))
+
+
+def join(own, came, bit):
+    return jnp.where(bit == 0, jnp.stack([own, came]), jnp.stack([came, own]))
+
+
+def gather_rows(values):
+    count = lax.axis_size("dp")
+    depth = count.bit_length() - 1
+    grp = lax.axis_index("grp")
+    width = values.shape[0]
+    padded = -(-width // 4096) * 4096
+    halves = jnp.pad(values, (0, padded - width)).reshape(2, 2, padded // 512, 128)
+    own = lax.dynamic_index_in_dim(halves, grp, 0, keepdims=False)
+    for position in range(2, depth)[::-1]:
+        own = join(own, swap(own, 1 << position), bit_of(position))
+    lead = own.ndim - 3
+    parts = [lax.index_in_dim(own, i, lead, keepdims=False) for i in (0, 1)]
+    for order in ((1, 0), (0, 1)):
+        for index in (0, 1):
+            position = order[index]
+            parts[index] = join(
+                parts[index], swap(parts[index], 1 << position), bit_of(position)
+            )
+    parts[1] = jnp.swapaxes(parts[1], 0, 1)
+    full = jnp.stack(parts, axis=depth)
+    full = full.transpose(tuple(range(depth))[::-1] + tuple(range(depth, full.ndim)))
+    full = full.reshape((count,) + full.shape[depth:])
+    other = swap(full, count)
+    whole = jnp.where(
+        grp == 0, jnp.stack([full, other], axis=1), jnp.stack([other, full], axis=1)
+    )
+    return whole.reshape(count, padded)[:, :width]
+
+
+def exchange_grads(front, back, factor):
+    gain_one, shift_one, qkv, qkv_bias, proj, proj_bias = front
+    gain_two, shift_two, fc1, fc1_bias, fc2, fc2_bias = back
+    count = lax.axis_size("dp")
+    rows = D // count
+    fc1_blocks = fc1.reshape(count, rows, 4, D).transpose(0, 2, 1, 3).reshape(count, 4 * rows, D)
+    fc2_blocks = fc2.reshape(count, 4 * rows, D)
+    mlp = (jnp.stack([fc1_blocks, fc2_blocks]) * factor).astype(jnp.bfloat16)
+    small = jnp.concatenate(
         [
-            lax.dynamic_slice_in_dim(weight_item.reshape(row_count, -1), own_index, 1, 0).astype(
-                jnp.float32
+            item.reshape(count, -1)
+            for item in (
+                gain_one,
+                shift_one,
+                qkv_bias,
+                proj_bias,
+                gain_two,
+                shift_two,
+                fc1_bias,
+                fc2_bias,
             )
-            for weight_item in weight_list
         ],
         axis=1,
     )
-    decay = jnp.concatenate(
-        [
-            jnp.full((1, weight_item.size // row_count), decay_flag, jnp.float32)
-            for weight_item, decay_flag in zip(weight_list, decay_flags)
-        ],
-        axis=1,
-    )
-    new_first = beta_one * first_moment + (1.0 - beta_one) * summed
-    new_second = beta_two * second_moment + (1.0 - beta_two) * summed * summed
-    ratio = (
-        new_first
-        / (1.0 - beta_one**step_count)
-        / (jnp.sqrt(new_second / (1.0 - beta_two**step_count)) + adam_eps)
-    )
-    fresh_low = (current - learn_rate * (ratio + decay_rate * decay * current)).astype(jnp.bfloat16)
-    new_weights = lax.all_gather(fresh_low, "dp", axis=0, tiled=True)
-    return (block_out, input_grad, summed, new_weights, new_first, new_second, summed_bias)
+    small = jnp.pad(small, ((0, 0), (0, D - small.shape[1])))[:, None]
+    small = jnp.pad(small, ((0, 0), (0, 7), (0, 0)))
+    qkv_blocks = qkv.reshape(count, rows, 3, D)
+    first_half = jnp.concatenate([qkv_blocks[:, :, 0], qkv_blocks[:, :, 1], small], axis=1)
+    second_half = jnp.concatenate(
+        [qkv_blocks[:, :, 2], proj.reshape(count, rows, D), jnp.zeros_like(small)], axis=1
+    )
+    rest = (jnp.stack([first_half, second_half]) * factor).astype(jnp.bfloat16)
+    return reduce_rows(mlp), reduce_rows(rest)
 
 
 def solution(mesh):

time: 1640 us -> 976 us (0.60)
  waiting for transfers between devices: 950 us -> 87.2 us
  other arithmetic: 106 us -> 222 us
  local copies, waits for them, and re-layouts: 272 us -> 335 us
  starting transfers between devices: 0.12 us -> 28.1 us
    unnamed x4 -> x0, waiting for transfers between devices: 667 us -> none
    all_gather x1 -> x0, waiting for transfers between devices: 283 us -> none  [on_device(): new_weights = lax.all_gather(fresh_low, 'dp', axis=0, tiled=True)]
    unnamed x215 -> x254, local copies, waits for them, and re-layouts: 188 us -> 62.4 us
    concatenate x6 -> x9, local copies, waits for them, and re-layouts: 4.23 us -> 92.6 us  [the longest x2 24.9 us: on_device(): current = jnp.concatenate(own_weights[lead:tail]).astype(jnp.float32)]
    ppermute x0 -> x30, waiting for transfers between devices: none -> 87.2 us  [swap(): return lax.ppermute(values, AXES, [(i, i ^ bit) for i in range(count)])]
    concatenate x0 -> x5, other arithmetic: none -> 35.9 us  [the longest x1 29 us: on_device(): new_weights = jnp.concatenate(fresh, axis=1)]
    convert_element_type x0 -> x16, other arithmetic: none -> 32.7 us  [the longest x12 19.8 us: add_low(): (kept.astype(jnp.float32) + came.astype(jnp.float32)).astype(jnp.bfloat16)]
    broadcast_in_dim x4 -> x9, local copies, waits for them, and re-layouts: 0.31 us -> 28.5 us  [the longest x1 9.01 us: on_device(): new_first = jnp.concatenate(first_out)[None]]
  transfers between devices with their start and end apart: 3 -> 30, of which waited for: 2 -> 11; matrix products, arithmetic and copies ran while one was open for 7% -> 32% of each run, Pallas kernels for 0% -> 0%
where the time goes in v1:
time: 976 us; the launch traced here: 962 us
  local copies, waits for them, and re-layouts  335 us (34%)
  matrix products  243 us (25%)
  other arithmetic  222 us (23%)
  waiting for transfers between devices  87.2 us (9%)
  blocking collectives  42.5 us (4%)
  starting transfers between devices  28.1 us (3%)
    ppermute x30, waiting for transfers between devices, swap(): return lax.ppermute(values, AXES, [(i, i ^ bit) for i in range(count)])  87.2 us
    unnamed x254, local copies, waits for them, and re-layouts  62.4 us
    psum x1, blocking collectives, on_device(): totals = lax.psum(member * images, ('grp', 'dp'))  42.5 us
    convert_element_type x1, other arithmetic, on_device(): grad_scores = (attn_probs * (grad_probs - jnp.sum(attn_probs * grad_probs...  41.9 us
    dot_general x2, matrix products, on_device(): jnp.einsum('qhd,khd->hqk', context_grad_part, value_rows, preferred_eleme...  39.7 us
    dot_general x2, matrix products, score_block(): jnp.einsum('qhd,khd->hqk', query_part, key_rows, preferred_element_type=j...  36.6 us
    dot_general x4, matrix products, contract_rows(): lax.dot_general(first_op, second_op, (((0,), (0,)), ((), ())), preferred_...  33.9 us
    dot_general x4, matrix products, contract_cols(): lax.dot_general(first_op, second_op, (((1,), (1,)), ((), ())), preferred_...  33.7 us
  transfers between devices with their start and end apart: 30, of which 11 were waited for; matrix products, arithmetic and copies ran while one was open for 32% of the time, Pallas kernels for 0%

profile of v1, /device:TPU:0, one launch (start us, length us, event | category | flops | bytes accessed | tf_op | source)
XLA Modules:
  0.0 962.1 jit_solution(8372519326813744182)
XLA Ops:
  28.9 12.1 %fusion.23 = (f32[12,512]{1,0:T(8,128)S(1)}, f32[12,512,1024]{2,1,0:T(8,128)}) fusion(pred[512,1024]{1,0:T(8,128)(4,1)S(1)} %get-tuple-element.141, bf16[512,12,64]{0,2,1:T(8,128)(2,1)} %bitcast.331, bf16[1024,12,64]{0,2,1:T(8,128)(2,1)S(1)} %bitcast.309), kind=kOutput, calls=%fused_computation.45 | convolution fusion | flops 824174592 | bytes 28073984 | tf_op jit(solution)/shard_map/qhd,khd->hqk/dot_general | solution.py:57
  41.1 12.3 %fusion.1 = f32[12,512]{1,0:T(8,128)S(1)} fusion(f32[12,512]{1,0:T(8,128)S(1)} %get-tuple-element.144, f32[12,512,1024]{2,1,0:T(8,128)} %get-tuple-element.145, pred[512,1024]{1,0:T(8,128)(4,1)} %copy-done.22), kind=kLoop, calls=%fused_computation.13 | loop fusion | flops 25159680 | bytes 25739264 | tf_op jit(solution)/shard_map/reduce_sum | solution.py:112
  66.4 24.5 %fusion.22 = (f32[12,512]{1,0:T(8,128)S(1)}, f32[12,512,1024]{2,1,0:T(8,128)}) fusion(pred[512,1024]{1,0:T(8,128)(4,1)} %get-tuple-element.140, bf16[512,12,64]{0,2,1:T(8,128)(2,1)} %bitcast.339, bf16[1024,12,64]{0,2,1:T(8,128)(2,1)S(1)} %bitcast.310), kind=kOutput, calls=%fused_computation.44 | convolution fusion | flops 824174592 | bytes 28073984 | tf_op jit(solution)/shard_map/qhd,khd->hqk/dot_general | solution.py:57
  90.9 13.4 %fusion = f32[12,512]{1,0:T(8,128)S(1)} fusion(f32[12,512]{1,0:T(8,128)S(1)} %get-tuple-element.146, f32[12,512,1024]{2,1,0:T(8,128)} %get-tuple-element.147, pred[512,1024]{1,0:T(8,128)(4,1)} %get-tuple-element.140), kind=kLoop, calls=%fused_computation.12 | loop fusion | flops 25159680 | bytes 25739264 | tf_op jit(solution)/shard_map/reduce_sum | solution.py:112
  129.0 17.5 %convert_reduce_fusion = (f32[3072]{0:T(1024)}, bf16[1024,3072]{1,0:T(8,128)(2,1)}) fusion(f32[1024,3072]{1,0:T(8,128)S(1)} %fusion.106, f32[3072]{0:T(1024)S(1)} %convert_element_type.315, bf16[3072,768]{1,0:T(8,128)(2,1)} %param.34, bf16[1024,768]{0,1:T(8,128)(2,1)S(1)} %copy.352, f32[1024]{0:T(1024)S(1)} %fusion.80), kind=kOutput, calls=%fused_computation.30 | convolution fusion | flops 4906546176 | bytes 25194496 | tf_op jit(solution)/shard_map/dot_general | solution.py:40
  168.3 13.2 %fusion.12 = f32[12,64,1024]{2,1,0:T(8,128)} fusion(bf16[512,12,64]{0,2,1:T(8,128)(2,1)S(1)} %bitcast.353, f32[12,512]{1,0:T(8,128)S(1)} %copy-done.82, f32[12,512,1024]{2,1,0:T(8,128)} %get-tuple-element.145, pred[512,1024]{1,0:T(8,128)(4,1)S(1)} %copy-done.23), kind=kOutput, calls=%fused_computation.28 | convolution fusion | flops 830472192 | bytes 29646848 | tf_op jit(solution)/shard_map/hqk,qhd->khd/dot_general | solution.py:190
  181.5 18.2 %multiply_reduce_fusion = (f32[12,512]{1,0:T(8,128)S(1)}, f32[12,512,1024]{2,1,0:T(8,128)}) fusion(f32[12,512]{1,0:T(8,128)S(1)} %copy-done.82, f32[12,512,1024]{2,1,0:T(8,128)} %get-tuple-element.145, pred[512,1024]{1,0:T(8,128)(4,1)S(1)} %copy-done.23, bf16[512,12,64]{0,2,1:T(8,128)(2,1)} %bitcast.354, bf16[1024,12,64]{0,2,1:T(8,128)(2,1)S(1)} %bitcast.324), kind=kOutput, calls=%fused_computation.1 | convolution fusion | flops 836757504 | bytes 53264384 | tf_op jit(solution)/shard_map/qhd,khd->hqk/dot_general | solution.py:173
  199.6 21.5 %multiply_reduce_fusion.1 = (f32[12,512]{1,0:T(8,128)S(1)}, f32[12,512,1024]{2,1,0:T(8,128)}) fusion(f32[12,512]{1,0:T(8,128)S(1)} %log_add_fusion.1, f32[12,512,1024]{2,1,0:T(8,128)} %get-tuple-element.147, pred[512,1024]{1,0:T(8,128)(4,1)S(1)} %copy-done.21, bf16[512,12,64]{0,2,1:T(8,128)(2,1)S(1)} %bitcast.351, bf16[1024,12,64]{0,2,1:T(8,128)(2,1)S(1)} %bitcast.325), kind=kOutput, calls=%fused_computation.4 | convolution fusion | flops 836757504 | bytes 53264384 | tf_op jit(solution)/shard_map/qhd,khd->hqk/dot_general | solution.py:173
  221.2 41.9 %multiply_convert_fusion = (bf16[12,512,1024]{2,1,0:T(8,128)(2,1)}, bf16[12,512,1024]{2,1,0:T(8,128)(2,1)}) fusion(f32[12,512,1024]{2,1,0:T(8,128)} %get-tuple-element.153, f32[12,512]{1,0:T(8,128)S(1)} %get-tuple-element.152, f32[12,512]{1,0:T(8,128)S(1)} %copy-done.82, f32[12,512,1024]{2,1,0:T(8,128)} %get-tuple-element.145, ...), kind=kLoop, calls=%fused_computation | loop fusion | flops 75497472 | bytes 126976000 | tf_op jit(solution)/shard_map/convert_element_type | solution.py:178
  281.5 14.4 %add_convert_fusion.2 = bf16[12,64,1024]{2,1,0:T(8,128)(2,1)} fusion(f32[12,64,1024]{2,1,0:T(8,128)} %fusion.12, bf16[512,12,64]{0,2,1:T(8,128)(2,1)} %bitcast.352, f32[12,512]{1,0:T(8,128)S(1)} %log_add_fusion.1, f32[12,512,1024]{2,1,0:T(8,128)} %get-tuple-element.147, pred[512,1024]{1,0:T(8,128)(4,1)} %get-tuple-element.140), kind=kOutput, calls=%fused_computation.76 | convolution fusion | flops 832045056 | bytes 31219712 | tf_op jit(solution)/shard_map/hqk,qhd->khd/dot_general | solution.py:190
  323.1 42.5 %psum.7 = s32[3]{0:T(128)S(1)} all-reduce(s32[3]{0:T(128)S(1)} %fusion.92), channel_id=1, replica_groups=mesh['grp'=2,'dp'=16] {'grp','dp'}, use_global_device_ids=true, to_apply=%region_26.27 | all-reduce | flops 3 | bytes 24 | tf_op jit(solution)/shard_map/psum | solution.py:87
  372.9 11.6 %reshape.935 = f32[16,48,3,768]{3,2,1,0:T(4,128)} reshape(f32[768,2304]{1,0:T(8,128)} %fusion.101) | data formatting | bytes 14155776 | tf_op jit(solution)/shard_map/reshape | solution.py:401
  384.5 13.0 %fusion.111 = (f32[16,48,1,768]{3,2,1,0:T(1,128)S(1)}, f32[16,48,1,768]{3,2,1,0:T(1,128)S(1)}, f32[16,48,1,768]{3,2,1,0:T(1,128)S(1)}) fusion(f32[16,48,3,768]{3,2,1,0:T(4,128)} %reshape.935), kind=kLoop, calls=%fused_computation.291 | loop fusion | bytes 14155776 | tf_op jit(solution)/shard_map/slice | solution.py:402
  425.6 14.9 %fusion.49 = f32[3072,768]{1,0:T(8,128)} fusion(bf16[1024,768]{0,1:T(8,128)(2,1)S(1)} %copy-done.19, f32[1024]{0:T(1024)S(1)} %fusion.80, f32[1024,3072]{1,0:T(8,128)} %copy-done.24, f32[3072]{0:T(1024)S(1)} %copy-done.96), kind=kOutput, calls=%fused_computation.113 | convolution fusion | flops 4865654784 | bytes 23609344 | tf_op jit(solution)/shard_map/dot_general | solution.py:34
  448.3 12.4 %reshape.947 = f32[16,48,4,768]{3,2,1,0:T(4,128)} reshape(f32[768,3072]{1,0:T(8,128)} %fusion.105) | data formatting | bytes 18874368 | tf_op jit(solution)/shard_map/reshape | solution.py:380
  488.6 12.7 %collective-permute-done.1 = bf16[2,2,2,52,768]{4,2,3,1,0:T(2,128)(2,1)} collective-permute-done((bf16[2,2,2,52,768]{4,2,3,1,0:T(2,128)(2,1)}, bf16[2,2,2,52,768]{4,2,3,1,0:T(2,128)(2,1)}, u32[]{:S(2)}, u32[]{:S(2)}) %collective-permute-start.1) | collective-permute-done | bytes 639008 | tf_op jit(solution)/shard_map/ppermute | solution.py:295
  508.0 12.6 %multiply_reduce_fusion.5 = (f32[295152]{0:T(1024)}, f32[295152]{0:T(1024)}) fusion(f32[1,442992]{1,0:T(1,128)S(1)} %copy-done.57, f32[1,442992]{1,0:T(1,128)S(1)} %copy-done.58), kind=kLoop, calls=%fused_computation.140 | loop fusion | flops 590304 | bytes 4722432 | tf_op jit(solution)/shard_map/mul | solution.py:268
  572.6 12.7 %concatenate.224 = f32[295152]{0:T(1024)} concatenate(f32[147456]{0:T(1024)} %broadcast.284, f32[192]{0:T(256)S(1)} %broadcast_in_dim.130, f32[147456]{0:T(1024)} %broadcast.284, f32[48]{0:T(128)S(1)} %broadcast.283), dimensions={0} | concatenate | bytes 2361216 | tf_op jit(solution)/shard_map/concatenate | solution.py:260
  587.3 10.3 %concatenate.221 = f32[147840]{0:T(1024)} concatenate(f32[96]{0:T(128)S(1)} %broadcast.282, f32[110592]{0:T(1024)} %broadcast_in_dim.127, f32[144]{0:T(256)} %broadcast_in_dim.128, f32[36864]{0:T(1024)} %broadcast_in_dim.129, f32[48]{0:T(128)S(1)} %broadcast.283, f32[96]{0:T(128)S(1)} %broadcast.282), dimensions={0} | concatenate | bytes 1182720 | tf_op jit(solution)/shard_map/concatenate | solution.py:260
  603.0 13.1 %concatenate.219 = bf16[147840]{0:T(1024)(128)(2,1)} concatenate(bf16[48]{0:T(256)(128)(2,1)} %get-tuple-element.164, bf16[48]{0:T(256)(128)(2,1)} %get-tuple-element.165, bf16[110592]{0:T(1024)(128)(2,1)} %dynamic-slice_reduce_fusion.2, bf16[144]{0:T(256)(128)(2,1)} %fusion.83, bf16[36864]{0:T(1024)(128)(2,1)S(1)} %dynamic-slice_reduce_fusion.3, ...), dimensions={0} | concatenate | bytes 591360 | tf_op jit(solution)/shard_map/concatenate | solution.py:259
  647.3 10.3 %concatenate.220 = f32[147840]{0:T(1024)} concatenate(f32[48]{0:T(128)S(1)} %get-tuple-element.127, f32[48]{0:T(128)S(1)} %get-tuple-element.126, f32[110592]{0:T(1024)} %reshape.946, f32[144]{0:T(256)S(1)} %bitcast.381, f32[36864]{0:T(1024)S(1)} %reshape_squeeze.9, f32[48]{0:T(128)S(1)} %get-tuple-element.125, f32[48]{0:T(128)S(1)} %get-tuple-element.124, f32[48]{0:T(128)S(1)} %get-tuple-element.123), dimensions={0} | concatenate | bytes 1182720 | tf_op jit(solution)/shard_map/concatenate | solution.py:258
  663.8 13.9 %collective-permute-done.14 = bf16[192,768]{1,0:T(8,128)(2,1)S(1)} collective-permute-done((bf16[192,768]{1,0:T(8,128)(2,1)S(1)}, bf16[192,768]{1,0:T(8,128)(2,1)S(1)}, u32[]{:S(2)}, u32[]{:S(2)}) %collective-permute-start.14) | collective-permute-done | bytes 294944 | tf_op jit(solution)/shard_map/ppermute | solution.py:295
  690.2 11.8 %concatenate.222 = bf16[295152]{0:T(1024)(128)(2,1)} concatenate(bf16[147456]{0:T(1024)(128)(2,1)} %get-tuple-element.163, bf16[192]{0:T(256)(128)(2,1)S(1)} %fusion.84, bf16[147456]{0:T(1024)(128)(2,1)} %get-tuple-element.162, bf16[48]{0:T(256)(128)(2,1)S(1)} %get-tuple-element.169), dimensions={0} | concatenate | bytes 1180608 | tf_op jit(solution)/shard_map/concatenate | solution.py:259
  715.0 12.9 %concatenate.223 = f32[295152]{0:T(1024)} concatenate(f32[147456]{0:T(1024)} %reshape.950, f32[192]{0:T(256)S(1)} %bitcast.379, f32[147456]{0:T(1024)} %reshape_squeeze.11, f32[48]{0:T(128)S(1)} %get-tuple-element.122), dimensions={0} | concatenate | bytes 2361216 | tf_op jit(solution)/shard_map/concatenate | solution.py:258
  738.6 10.7 %collective-permute-done.23 = bf16[2,584,128]{2,1,0:T(8,128)(2,1)S(1)} collective-permute-done((bf16[2,584,128]{2,1,0:T(8,128)(2,1)S(1)}, bf16[2,584,128]{2,1,0:T(8,128)(2,1)S(1)}, u32[]{:S(2)}, u32[]{:S(2)}) %collective-permute-start.23) | collective-permute-done | bytes 299040 | tf_op jit(solution)/shard_map/ppermute | solution.py:295
  750.4 10.4 %add_convert_fusion.3 = bf16[1024,768]{0,1:T(8,128)(2,1)} fusion(f32[1024,768]{0,1:T(8,128)S(1)} %copy-done.6, bf16[3072,768]{1,0:T(8,128)(2,1)S(1)} %bitcast.347, f32[768]{0:T(1024)S(1)} %copy-done.107, f32[1024,3072]{1,0:T(8,128)} %copy-done.24, f32[3072]{0:T(1024)S(1)} %copy-done.97), kind=kOutput, calls=%fused_computation.83 | convolution fusion | flops 4865654784 | bytes 22035456 | tf_op jit(solution)/shard_map/dot_general | solution.py:140
  799.8 22.0 %collective-permute-done.28 = bf16[2,2,2,584,128]{4,3,2,1,0:T(8,128)(2,1)S(1)} collective-permute-done((bf16[2,2,2,584,128]{4,3,2,1,0:T(8,128)(2,1)S(1)}, bf16[2,2,2,584,128]{4,3,2,1,0:T(8,128)(2,1)S(1)}, u32[]{:S(2)}, u32[]{:S(2)}) %collective-permute-start.28) | collective-permute-done | bytes 1196064 | tf_op jit(solution)/shard_map/ppermute | solution.py:295
  828.3 21.3 %concatenate.218 = f32[442992]{0:T(1024)} concatenate(f32[48]{0:T(128)S(1)} %get-tuple-element.127, f32[48]{0:T(128)S(1)} %get-tuple-element.126, f32[110592]{0:T(1024)S(1)} %copy-done.37, f32[144]{0:T(256)S(1)} %bitcast.382, f32[36864]{0:T(1024)} %copy-done.63, f32[48]{0:T(128)S(1)} %get-tuple-element.125, f32[48]{0:T(128)S(1)} %get-tuple-element.124, ...), dimensions={0} | concatenate | bytes 3543936 | tf_op jit(solution)/shard_map/concatenate | solution.py:282
  879.5 13.1 %copy.430 = bf16[2,8,1184,128]{3,1,2,0:T(8,128)(2,1)S(1)} copy(bf16[2,8,1184,128]{3,2,1,0:T(8,128)(2,1)S(1)} %bitcast.316) | data formatting | bytes 9699328
  895.0 11.7 %maximum_select_fusion = bf16[16,2,2,584,128]{4,3,2,0,1:T(8,128)(2,1)} fusion(bf16[16,1,2,584,128]{4,3,2,0,1:T(8,128)(2,1)} %bitcast.132, bf16[16,1,2,584,128]{4,3,2,0,1:T(8,128)(2,1)} %bitcast.130, pred[]{:T(512)S(6)} %eq.37), kind=kLoop, calls=%fused_computation.39 | loop fusion | flops 14352384 | bytes 19136512 | tf_op jit(solution)/shard_map/jit(_where)/select_n | solution.py:369
  914.8 17.4 %copy.429 = bf16[2,8,2336,128]{3,1,2,0:T(8,128)(2,1)S(1)} copy(bf16[2,8,2336,128]{3,2,1,0:T(8,128)(2,1)} %bitcast.313) | data formatting | bytes 19136512
  933.0 29.0 %pad_maximum_fusion = bf16[16,442992]{1,0:T(8,128)(2,1)} fusion(bf16[16,295152]{1,0:T(8,128)(2,1)S(1)} %slice.256, bf16[16,147840]{1,0:T(8,128)(2,1)S(1)} %bitcast.319), kind=kLoop, calls=%fused_computation.20 | loop fusion | flops 28351488 | bytes 28351488 | tf_op jit(solution)/shard_map/concatenate | solution.py:285
  (514 shorter events, 428.4 us)
Async XLA Ops:
  7.1 112.8 %copy-start.2 = (bf16[1024,768]{0,1:T(8,128)(2,1)}, bf16[1024,768]{0,1:T(8,128)(2,1)S(1)}, u32[]{:S(2)}) copy-start(bf16[1024,768]{0,1:T(8,128)(2,1)S(1)} %copy.346) | copy-start | bytes 4718596
  425.2 51.6 %collective-permute-start = (bf16[16,104,768]{2,1,0:T(8,128)(2,1)}, bf16[16,104,768]{2,1,0:T(8,128)(2,1)}, u32[]{:S(2)}, u32[]{:S(2)}) collective-permute-start(bf16[16,104,768]{2,1,0:T(8,128)(2,1)} %dynamic-slice_bitcast_fusion.1), channel_id=1, source_target_pairs={{0,16},{1,17},{2,18},{3,19},{4,20},{5,21},{6,22},{7,23},{8,24},{9,... | collective-permute-start | bytes 7667720 | tf_op jit(solution)/shard_map/ppermute | solution.py:295
  476.7 46.8 %collective-permute-start.8 = (bf16[16,192,768]{2,1,0:T(8,128)(2,1)}, bf16[16,192,768]{2,1,0:T(8,128)(2,1)}, u32[]{:S(2)}, u32[]{:S(2)}) collective-permute-start(bf16[16,192,768]{2,1,0:T(8,128)(2,1)} %dynamic-slice_bitcast_fusion), channel_id=1, source_target_pairs={{0,16},{1,17},{2,18},{3,19},{4,20},{5,21},{6,22},{7,23},{8,24},{9,... | collective-permute-start | bytes 14155784 | tf_op jit(solution)/shard_map/ppermute | solution.py:295
  483.7 17.6 %collective-permute-start.1 = (bf16[2,2,2,52,768]{4,2,3,1,0:T(2,128)(2,1)}, bf16[2,2,2,52,768]{4,2,3,1,0:T(2,128)(2,1)}, u32[]{:S(2)}, u32[]{:S(2)}) collective-permute-start(bf16[2,2,2,52,768]{4,2,3,1,0:T(2,128)(2,1)} %bitcast.301), channel_id=1, source_target_pairs={{0,1},{1,0},{2,3},{3,2},{4,5},{5,4},{6,7},{7,6},{8,9},{9,8},{10,11... | collective-permute-start | bytes 1916936 | tf_op jit(solution)/shard_map/ppermute | solution.py:295
  487.9 17.8 %collective-permute-start.3 = (bf16[2,2,2,52,768]{4,2,3,1,0:T(2,128)(2,1)S(1)}, bf16[2,2,2,52,768]{4,2,3,1,0:T(2,128)(2,1)S(1)}, u32[]{:S(2)}, u32[]{:S(2)}) collective-permute-start(bf16[2,2,2,52,768]{4,2,3,1,0:T(2,128)(2,1)S(1)} %bitcast.373), channel_id=1, source_target_pairs={{0,2},{1,3},{2,0},{3,1},{4,6},{5,7},{6,4},{7,5},{8,10},{9,11},{10,... | collective-permute-start | bytes 1916936 | tf_op jit(solution)/shard_map/ppermute | solution.py:295
  504.0 16.7 %collective-permute-start.2 = (bf16[2,2,52,768]{3,1,2,0:T(2,128)(2,1)}, bf16[2,2,52,768]{3,1,2,0:T(2,128)(2,1)S(1)}, u32[]{:S(2)}, u32[]{:S(2)}) collective-permute-start(bf16[2,2,52,768]{3,1,2,0:T(2,128)(2,1)} %dynamic-slice_bitcast_fusion.5), channel_id=1, source_target_pairs={{0,2},{1,3},{2,0},{3,1},{4,6},{5,7},{6,4},{7,5},{8,10},{9,11},{10,... | collective-permute-start | bytes 958472 | tf_op jit(solution)/shard_map/ppermute | solution.py:295
  507.4 14.7 %collective-permute-start.4 = (bf16[2,2,52,768]{3,1,2,0:T(2,128)(2,1)}, bf16[2,2,52,768]{3,1,2,0:T(2,128)(2,1)}, u32[]{:S(2)}, u32[]{:S(2)}) collective-permute-start(bf16[2,2,52,768]{3,1,2,0:T(2,128)(2,1)} %dynamic-slice_bitcast_fusion.4), channel_id=1, source_target_pairs={{0,1},{1,0},{2,3},{3,2},{4,5},{5,4},{6,7},{7,6},{8,9},{9,8},{10,11... | collective-permute-start | bytes 958472 | tf_op jit(solution)/shard_map/ppermute | solution.py:295
  532.6 84.7 %collective-permute-start.9 = (bf16[2,2,2,96,768]{4,3,0,1,2:T(8,128)(2,1)}, bf16[2,2,2,96,768]{4,3,0,1,2:T(8,128)(2,1)}, u32[]{:S(2)}, u32[]{:S(2)}) collective-permute-start(bf16[2,2,2,96,768]{4,3,0,1,2:T(8,128)(2,1)} %bitcast.300), channel_id=1, source_target_pairs={{0,1},{1,0},{2,3},{3,2},{4,5},{5,4},{6,7},{7,6},{8,9},{9,8},{10,11... | collective-permute-start | bytes 3538952 | tf_op jit(solution)/shard_map/ppermute | solution.py:295
  537.2 9.5 collective-permute-start.5
  546.5 74.6 %collective-permute-start.11 = (bf16[2,2,2,96,768]{4,3,0,1,2:T(8,128)(2,1)}, bf16[2,2,2,96,768]{4,3,0,1,2:T(8,128)(2,1)}, u32[]{:S(2)}, u32[]{:S(2)}) collective-permute-start(bf16[2,2,2,96,768]{4,3,0,1,2:T(8,128)(2,1)} %bitcast.299), channel_id=1, source_target_pairs={{0,2},{1,3},{2,0},{3,1},{4,6},{5,7},{6,4},{7,5},{8,10},{9,11},{10,... | collective-permute-start | bytes 3538952 | tf_op jit(solution)/shard_map/ppermute | solution.py:295
  549.2 67.0 %collective-permute-start.6 = (bf16[104,768]{1,0:T(8,128)(2,1)}, bf16[104,768]{1,0:T(8,128)(2,1)}, u32[]{:S(2)}, u32[]{:S(2)}) collective-permute-start(bf16[104,768]{1,0:T(8,128)(2,1)} %dynamic-slice_bitcast_fusion.7), channel_id=1, source_target_pairs={{0,8},{1,9},{2,10},{3,11},{4,12},{5,13},{6,14},{7,15},{8,0},{9,1},... | collective-permute-start | bytes 479240 | tf_op jit(solution)/shard_map/ppermute | solution.py:295
  617.2 14.3 %collective-permute-start.7 = (f32[104,768]{1,0:T(8,128)S(1)}, f32[104,768]{1,0:T(8,128)S(1)}, u32[]{:S(2)}, u32[]{:S(2)}) collective-permute-start(f32[104,768]{1,0:T(8,128)S(1)} %convert_add_fusion.13), channel_id=1, source_target_pairs={{0,16},{1,17},{2,18},{3,19},{4,20},{5,21},{6,22},{7,23},{8,24},{9,... | collective-permute-start | bytes 958472 | tf_op jit(solution)/shard_map/ppermute | solution.py:295
  619.3 15.8 %collective-permute-start.10 = (bf16[2,2,96,768]{3,2,0,1:T(8,128)(2,1)S(1)}, bf16[2,2,96,768]{3,2,0,1:T(8,128)(2,1)S(1)}, u32[]{:S(2)}, u32[]{:S(2)}) collective-permute-start(bf16[2,2,96,768]{3,2,0,1:T(8,128)(2,1)S(1)} %dynamic-slice_bitcast_fusion.3), channel_id=1, source_target_pairs={{0,2},{1,3},{2,0},{3,1},{4,6},{5,7},{6,4},{7,5},{8,10},{9,11},{10,... | collective-permute-start | bytes 1769480 | tf_op jit(solution)/shard_map/ppermute | solution.py:295
  622.7 15.5 %collective-permute-start.12 = (bf16[2,2,96,768]{3,2,0,1:T(8,128)(2,1)S(1)}, bf16[2,2,96,768]{3,2,0,1:T(8,128)(2,1)S(1)}, u32[]{:S(2)}, u32[]{:S(2)}) collective-permute-start(bf16[2,2,96,768]{3,2,0,1:T(8,128)(2,1)S(1)} %dynamic-slice_bitcast_fusion.2), channel_id=1, source_target_pairs={{0,1},{1,0},{2,3},{3,2},{4,5},{5,4},{6,7},{7,6},{8,9},{9,8},{10,11... | collective-permute-start | bytes 1769480 | tf_op jit(solution)/shard_map/ppermute | solution.py:295
  639.4 18.2 %collective-permute-start.13 = (bf16[2,192,768]{2,1,0:T(8,128)(2,1)}, bf16[2,192,768]{2,1,0:T(8,128)(2,1)}, u32[]{:S(2)}, u32[]{:S(2)}) collective-permute-start(bf16[2,192,768]{2,1,0:T(8,128)(2,1)} %fusion.76), channel_id=1, source_target_pairs={{0,4},{1,5},{2,6},{3,7},{4,0},{5,1},{6,2},{7,3},{8,12},{9,13},{10,... | collective-permute-start | bytes 1769480 | tf_op jit(solution)/shard_map/ppermute | solution.py:295
  647.3 180.8 %copy-start.105 = (f32[48]{0:T(128)}, f32[48]{0:T(128)S(1)}, u32[]{:S(2)}) copy-start(f32[48]{0:T(128)S(1)} %get-tuple-element.122) | copy-start | bytes 580
  659.1 18.5 %collective-permute-start.14 = (bf16[192,768]{1,0:T(8,128)(2,1)S(1)}, bf16[192,768]{1,0:T(8,128)(2,1)S(1)}, u32[]{:S(2)}, u32[]{:S(2)}) collective-permute-start(bf16[192,768]{1,0:T(8,128)(2,1)S(1)} %dynamic-slice_bitcast_fusion.6), channel_id=1, source_target_pairs={{0,8},{1,9},{2,10},{3,11},{4,12},{5,13},{6,14},{7,15},{8,0},{9,1},... | collective-permute-start | bytes 884744 | tf_op jit(solution)/shard_map/ppermute | solution.py:295
  661.4 19.4 %collective-permute-start.16 = (bf16[2,296,128]{2,1,0:T(8,128)(2,1)S(1)}, bf16[2,296,128]{2,1,0:T(8,128)(2,1)S(1)}, u32[]{:S(2)}, u32[]{:S(2)}) collective-permute-start(bf16[2,296,128]{2,1,0:T(8,128)(2,1)S(1)} %fusion.158), channel_id=1, source_target_pairs={{0,8},{1,9},{2,10},{3,11},{4,12},{5,13},{6,14},{7,15},{8,0},{9,1},... | collective-permute-start | bytes 454664 | tf_op jit(solution)/shard_map/ppermute | solution.py:295
  678.6 27.3 %collective-permute-start.15 = (f32[192,768]{1,0:T(8,128)}, f32[192,768]{1,0:T(8,128)}, u32[]{:S(2)}, u32[]{:S(2)}) collective-permute-start(f32[192,768]{1,0:T(8,128)} %convert_add_fusion.12), channel_id=1, source_target_pairs={{0,16},{1,17},{2,18},{3,19},{4,20},{5,21},{6,22},{7,23},{8,24},{9,... | collective-permute-start | bytes 1769480 | tf_op jit(solution)/shard_map/ppermute | solution.py:295
  681.6 22.2 %collective-permute-start.17 = (bf16[2,2,296,128]{3,2,1,0:T(8,128)(2,1)}, bf16[2,2,296,128]{3,2,1,0:T(8,128)(2,1)}, u32[]{:S(2)}, u32[]{:S(2)}) collective-permute-start(bf16[2,2,296,128]{3,2,1,0:T(8,128)(2,1)} %maximum_select_fusion.21), channel_id=1, source_target_pairs={{0,4},{1,5},{2,6},{3,7},{4,0},{5,1},{6,2},{7,3},{8,12},{9,13},{10,... | collective-permute-start | bytes 909320 | tf_op jit(solution)/shard_map/ppermute | solution.py:295
  733.0 16.4 %collective-permute-start.23 = (bf16[2,584,128]{2,1,0:T(8,128)(2,1)S(1)}, bf16[2,584,128]{2,1,0:T(8,128)(2,1)S(1)}, u32[]{:S(2)}, u32[]{:S(2)}) collective-permute-start(bf16[2,584,128]{2,1,0:T(8,128)(2,1)S(1)} %fusion.160), channel_id=1, source_target_pairs={{0,8},{1,9},{2,10},{3,11},{4,12},{5,13},{6,14},{7,15},{8,0},{9,1},... | collective-permute-start | bytes 897032 | tf_op jit(solution)/shard_map/ppermute | solution.py:295
  736.6 30.1 %collective-permute-start.18 = (bf16[2,2,296,128]{3,2,1,0:T(8,128)(2,1)}, bf16[2,2,296,128]{3,2,1,0:T(8,128)(2,1)}, u32[]{:S(2)}, u32[]{:S(2)}) collective-permute-start(bf16[2,2,296,128]{3,2,1,0:T(8,128)(2,1)} %get-tuple-element.135), channel_id=1, source_target_pairs={{0,2},{1,3},{2,0},{3,1},{4,6},{5,7},{6,4},{7,5},{8,10},{9,11},{10,... | collective-permute-start | bytes 909320 | tf_op jit(solution)/shard_map/ppermute | solution.py:295
  736.9 28.2 %collective-permute-start.20 = (bf16[2,2,296,128]{3,2,1,0:T(8,128)(2,1)}, bf16[2,2,296,128]{3,2,1,0:T(8,128)(2,1)}, u32[]{:S(2)}, u32[]{:S(2)}) collective-permute-start(bf16[2,2,296,128]{3,2,1,0:T(8,128)(2,1)} %get-tuple-element.136), channel_id=1, source_target_pairs={{0,1},{1,0},{2,3},{3,2},{4,5},{5,4},{6,7},{7,6},{8,9},{9,8},{10,11... | collective-permute-start | bytes 909320 | tf_op jit(solution)/shard_map/ppermute | solution.py:295
  750.3 19.5 %collective-permute-start.24 = (bf16[2,2,584,128]{3,2,1,0:T(8,128)(2,1)}, bf16[2,2,584,128]{3,2,1,0:T(8,128)(2,1)}, u32[]{:S(2)}, u32[]{:S(2)}) collective-permute-start(bf16[2,2,584,128]{3,2,1,0:T(8,128)(2,1)} %maximum_select_fusion.19), channel_id=1, source_target_pairs={{0,4},{1,5},{2,6},{3,7},{4,0},{5,1},{6,2},{7,3},{8,12},{9,13},{10,... | collective-permute-start | bytes 1794056 | tf_op jit(solution)/shard_map/ppermute | solution.py:295
  766.3 16.7 %collective-permute-start.21 = (bf16[2,2,2,296,128]{4,3,2,1,0:T(8,128)(2,1)S(1)}, bf16[2,2,2,296,128]{4,3,2,1,0:T(8,128)(2,1)S(1)}, u32[]{:S(2)}, u32[]{:S(2)}) collective-permute-start(bf16[2,2,2,296,128]{4,3,2,1,0:T(8,128)(2,1)S(1)} %maximum_select_fusion.17), channel_id=1, source_target_pairs={{0,2},{1,3},{2,0},{3,1},{4,6},{5,7},{6,4},{7,5},{8,10},{9,11},{10,... | collective-permute-start | bytes 1818632 | tf_op jit(solution)/shard_map/ppermute | solution.py:295
  767.9 16.7 %collective-permute-start.19 = (bf16[2,2,2,296,128]{4,3,2,1,0:T(8,128)(2,1)S(1)}, bf16[2,2,2,296,128]{4,3,2,1,0:T(8,128)(2,1)S(1)}, u32[]{:S(2)}, u32[]{:S(2)}) collective-permute-start(bf16[2,2,2,296,128]{4,3,2,1,0:T(8,128)(2,1)S(1)} %maximum_select_fusion.15), channel_id=1, source_target_pairs={{0,1},{1,0},{2,3},{3,2},{4,5},{5,4},{6,7},{7,6},{8,9},{9,8},{10,11... | collective-permute-start | bytes 1818632 | tf_op jit(solution)/shard_map/ppermute | solution.py:295
  771.8 23.5 %collective-permute-start.27 = (bf16[2,2,584,128]{3,2,1,0:T(8,128)(2,1)S(1)}, bf16[2,2,584,128]{3,2,1,0:T(8,128)(2,1)S(1)}, u32[]{:S(2)}, u32[]{:S(2)}) collective-permute-start(bf16[2,2,584,128]{3,2,1,0:T(8,128)(2,1)S(1)} %get-tuple-element.116), channel_id=1, source_target_pairs={{0,1},{1,0},{2,3},{3,2},{4,5},{5,4},{6,7},{7,6},{8,9},{9,8},{10,11... | collective-permute-start | bytes 1794056 | tf_op jit(solution)/shard_map/ppermute | solution.py:295
  774.6 22.6 %collective-permute-start.25 = (bf16[2,2,584,128]{3,2,1,0:T(8,128)(2,1)S(1)}, bf16[2,2,584,128]{3,2,1,0:T(8,128)(2,1)S(1)}, u32[]{:S(2)}, u32[]{:S(2)}) collective-permute-start(bf16[2,2,584,128]{3,2,1,0:T(8,128)(2,1)S(1)} %get-tuple-element.115), channel_id=1, source_target_pairs={{0,2},{1,3},{2,0},{3,1},{4,6},{5,7},{6,4},{7,5},{8,10},{9,11},{10,... | collective-permute-start | bytes 1794056 | tf_op jit(solution)/shard_map/ppermute | solution.py:295
  785.2 90.8 %collective-permute-start.22 = (bf16[16,2,296,128]{3,2,1,0:T(8,128)(2,1)S(1)}, bf16[16,2,296,128]{3,2,1,0:T(8,128)(2,1)}, u32[]{:S(2)}, u32[]{:S(2)}) collective-permute-start(bf16[16,2,296,128]{3,2,1,0:T(8,128)(2,1)S(1)} %bitcast.329), channel_id=1, source_target_pairs={{0,16},{1,17},{2,18},{3,19},{4,20},{5,21},{6,22},{7,23},{8,24},{9,... | collective-permute-start | bytes 7274504 | tf_op jit(solution)/shard_map/ppermute | solution.py:295
  795.5 26.3 %collective-permute-start.28 = (bf16[2,2,2,584,128]{4,3,2,1,0:T(8,128)(2,1)S(1)}, bf16[2,2,2,584,128]{4,3,2,1,0:T(8,128)(2,1)S(1)}, u32[]{:S(2)}, u32[]{:S(2)}) collective-permute-start(bf16[2,2,2,584,128]{4,3,2,1,0:T(8,128)(2,1)S(1)} %maximum_select_fusion.10), channel_id=1, source_target_pairs={{0,2},{1,3},{2,0},{3,1},{4,6},{5,7},{6,4},{7,5},{8,10},{9,11},{10,... | collective-permute-start | bytes 3588104 | tf_op jit(solution)/shard_map/ppermute | solution.py:295
  797.4 26.0 %collective-permute-start.26 = (bf16[2,2,2,584,128]{4,3,2,1,0:T(8,128)(2,1)S(1)}, bf16[2,2,2,584,128]{4,3,2,1,0:T(8,128)(2,1)S(1)}, u32[]{:S(2)}, u32[]{:S(2)}) collective-permute-start(bf16[2,2,2,584,128]{4,3,2,1,0:T(8,128)(2,1)S(1)} %maximum_select_fusion.8), channel_id=1, source_target_pairs={{0,1},{1,0},{2,3},{3,2},{4,5},{5,4},{6,7},{7,6},{8,9},{9,8},{10,11... | collective-permute-start | bytes 3588104 | tf_op jit(solution)/shard_map/ppermute | solution.py:295
  826.8 68.2 %collective-permute-start.29 = (bf16[16,2,584,128]{3,2,1,0:T(8,128)(2,1)}, bf16[16,2,584,128]{3,2,1,0:T(8,128)(2,1)}, u32[]{:S(2)}, u32[]{:S(2)}) collective-permute-start(bf16[16,2,584,128]{3,2,1,0:T(8,128)(2,1)} %bitcast.131), channel_id=1, source_target_pairs={{0,16},{1,17},{2,18},{3,19},{4,20},{5,21},{6,22},{7,23},{8,24},{9,... | collective-permute-start | bytes 14352392 | tf_op jit(solution)/shard_map/ppermute | solution.py:295
  (120 other events, 1378.5 us)

commit v2 on v1

--- a/solution.py
+++ b/solution.py
@@ -1,6 +1,8 @@
 import jax
 import jax.numpy as jnp
 from jax import lax
+from jax.experimental import pallas as pl
+from jax.experimental.pallas import tpu as pltpu
 from jax.sharding import PartitionSpec as P
 
 D = 768
@@ -52,11 +54,201 @@
     return (segment, position < segment_ends[-1])
 
 
-def score_block(query_part, key_rows, same_segment):
-    raw = (
-        jnp.einsum("qhd,khd->hqk", query_part, key_rows, preferred_element_type=jnp.float32) * 0.125
-    )
-    return jnp.where(same_segment[None], raw, neg_fill)
+TILE = 128
+WINDOW = 3 * TILE
+
+
+def window_start(tile, tiles):
+    return min(max(tile - 1, 0), tiles - 3) * TILE
+
+
+def dot_nt(first, second):
+    return lax.dot_general(first, second, (((1,), (1,)), ((), ())), preferred_element_type=jnp.float32)
+
+
+def dot_tn(first, second):
+    return lax.dot_general(first, second, (((0,), (0,)), ((), ())), preferred_element_type=jnp.float32)
+
+
+def dot_nn(first, second):
+    return jnp.dot(first, second, preferred_element_type=jnp.float32)
+
+
+def stack_heads(block, low):
+    zero = jnp.zeros_like(block)
+    return jnp.concatenate([jnp.where(low, block, zero), jnp.where(low, zero, block)], axis=0)
+
+
+def merge_heads(block, low):
+    return jnp.where(low, block[:TILE], block[TILE:])
+
+
+def fill_masks(bias_ref, seg_col_ref, seg_row_ref, tiles):
+    for tile in range(tiles):
+        start = window_start(tile, tiles)
+        same = (
+            seg_col_ref[tile * TILE : (tile + 1) * TILE, :]
+            == seg_row_ref[:, start : start + WINDOW]
+        )
+        bias_ref[tile] = jnp.where(same, 0.0, neg_fill)
+
+
+def soft_probs(scores):
+    row_max = jnp.max(scores, axis=1, keepdims=True)
+    exponent = jnp.exp(scores - row_max)
+    return exponent * (1.0 / jnp.sum(exponent, axis=1, keepdims=True))
+
+
+def attn_forward_kernel(
+    pad_ref, query_ref, key_ref, value_ref, seg_col_ref, seg_row_ref, out_ref, bias_ref
+):
+    length = query_ref.shape[0]
+    tiles = length // TILE
+
+    @pl.when(pl.program_id(0) == 0)
+    def _():
+        fill_masks(bias_ref, seg_col_ref, seg_row_ref, tiles)
+
+    low = lax.broadcasted_iota(jnp.int32, (TILE, 128), 1) < 64
+    scale = jnp.asarray(0.125, jnp.bfloat16)
+
+    for tile in range(tiles):
+        start = window_start(tile, tiles)
+        queries = stack_heads(query_ref[tile * TILE : (tile + 1) * TILE, :] * scale, low)
+        bias = bias_ref[tile]
+        scores = dot_nt(queries, key_ref[start : start + WINDOW, :]) + jnp.concatenate(
+            [bias, bias], axis=0
+        )
+        probs = soft_probs(scores).astype(jnp.bfloat16)
+        mixed = dot_nn(probs, value_ref[start : start + WINDOW, :])
+        out_ref[tile * TILE : (tile + 1) * TILE, :] = merge_heads(mixed, low).astype(jnp.bfloat16)
+
+    @pl.loop(0, tiles)
+    def _(tile):
+        start = jnp.minimum(jnp.maximum(tile - 1, 0), tiles - 3) * TILE
+        padding = (tile + 1) * TILE > pad_ref[0]
+        outside = (pad_ref[0] < start) | (start + WINDOW < length)
+
+        @pl.when(padding & outside)
+        def _():
+            rows = pl.ds(pl.multiple_of(tile * TILE, TILE), TILE)
+            queries = stack_heads(query_ref[rows, :] * scale, low)
+            same = seg_col_ref[rows, :] == seg_row_ref[...]
+            bias = jnp.where(same, 0.0, neg_fill)
+            scores = dot_nt(queries, key_ref[...]) + jnp.concatenate([bias, bias], axis=0)
+            probs = soft_probs(scores).astype(jnp.bfloat16)
+            out_ref[rows, :] = merge_heads(dot_nn(probs, value_ref[...]), low).astype(jnp.bfloat16)
+
+
+def attn_forward(projected, seg_col, seg_row, pad_start):
+    length, width = projected.shape
+    pairs = width // 3 // 128
+    tiles = length // TILE
+
+    def part(offset):
+        return pl.BlockSpec((length, 128), lambda pair, pad: (0, offset * pairs + pair))
+
+    return pl.pallas_call(
+        attn_forward_kernel,
+        out_shape=jax.ShapeDtypeStruct((length, width // 3), jnp.bfloat16),
+        grid_spec=pltpu.PrefetchScalarGridSpec(
+            num_scalar_prefetch=1,
+            grid=(pairs,),
+            in_specs=[
+                part(0),
+                part(1),
+                part(2),
+                pl.BlockSpec((length, 1), lambda pair, pad: (0, 0)),
+                pl.BlockSpec((1, length), lambda pair, pad: (0, 0)),
+            ],
+            out_specs=pl.BlockSpec((length, 128), lambda pair, pad: (0, pair)),
+            scratch_shapes=[pltpu.VMEM((tiles, TILE, WINDOW), jnp.float32)],
+        ),
+        compiler_params=pltpu.CompilerParams(vmem_limit_bytes=40 * 2**20),
+        cost_estimate=pl.CostEstimate(
+            flops=4 * length * WINDOW * width // 3,
+            bytes_accessed=8 * length * width // 3,
+            transcendentals=length * WINDOW * 12,
+        ),
+        name="attn_forward",
+    )(pad_start, projected, projected, projected, seg_col, seg_row)
+
+
+def attn_backward_kernel(
+    query_ref, key_ref, value_ref, grad_ref, seg_col_ref, seg_row_ref,
+    query_out, key_out, value_out, bias_ref, key_sum, value_sum,
+):
+    length = query_ref.shape[0]
+    tiles = length // TILE
+
+    @pl.when(pl.program_id(0) == 0)
+    def _():
+        fill_masks(bias_ref, seg_col_ref, seg_row_ref, tiles)
+
+    low = lax.broadcasted_iota(jnp.int32, (TILE, 128), 1) < 64
+    scale = jnp.asarray(0.125, jnp.bfloat16)
+    key_sum[...] = jnp.zeros_like(key_sum)
+    value_sum[...] = jnp.zeros_like(value_sum)
+
+    for tile in range(tiles):
+        start = window_start(tile, tiles)
+        rows = slice(tile * TILE, (tile + 1) * TILE)
+        span = slice(start, start + WINDOW)
+        queries = stack_heads(query_ref[rows, :] * scale, low)
+        grads = stack_heads(grad_ref[rows, :], low)
+        bias = bias_ref[tile]
+        keys = key_ref[span, :]
+        scores = dot_nt(queries, keys) + jnp.concatenate([bias, bias], axis=0)
+        probs = soft_probs(scores)
+        grad_probs = dot_nt(grads, value_ref[span, :])
+        delta = jnp.sum(probs * grad_probs, axis=1, keepdims=True)
+        grad_scores = (probs * (grad_probs - delta)).astype(jnp.bfloat16)
+        query_out[rows, :] = (merge_heads(dot_nn(grad_scores, keys), low) * 0.125).astype(
+            jnp.bfloat16
+        )
+        key_sum[span, :] += dot_tn(grad_scores, queries)
+        value_sum[span, :] += dot_tn(probs.astype(jnp.bfloat16), grads)
+    key_out[...] = key_sum[...].astype(jnp.bfloat16)
+    value_out[...] = value_sum[...].astype(jnp.bfloat16)
+
+
+def attn_backward(projected, grad_context, seg_col, seg_row):
+    length, width = projected.shape
+    pairs = width // 3 // 128
+    tiles = length // TILE
+
+    def part(offset):
+        return pl.BlockSpec((length, 128), lambda pair: (0, offset * pairs + pair))
+
+    return pl.pallas_call(
+        attn_backward_kernel,
+        out_shape=[jax.ShapeDtypeStruct((length, width // 3), jnp.bfloat16)] * 3,
+        grid_spec=pltpu.PrefetchScalarGridSpec(
+            num_scalar_prefetch=0,
+            grid=(pairs,),
+            in_specs=[
+                part(0),
+                part(1),
+                part(2),
+                part(0),
+                pl.BlockSpec((length, 1), lambda pair: (0, 0)),
+                pl.BlockSpec((1, length), lambda pair: (0, 0)),
+            ],
+            out_specs=[part(0)] * 3,
+            scratch_shapes=[
+                pltpu.VMEM((tiles, TILE, WINDOW), jnp.float32),
+                pltpu.VMEM((length, 128), jnp.float32),
+                pltpu.VMEM((length, 128), jnp.float32),
+            ],
+        ),
+        compiler_params=pltpu.CompilerParams(vmem_limit_bytes=40 * 2**20),
+        cost_estimate=pl.CostEstimate(
+            flops=10 * length * WINDOW * width // 3,
+            bytes_accessed=14 * length * width // 3,
+            transcendentals=length * WINDOW * 12,
+        ),
+        name="attn_backward",
+    )(projected, projected, projected, grad_context, seg_col, seg_row)
 
 
 def on_device(
@@ -84,7 +276,9 @@
     segment, valid_rows = segment_info(image_counts[0], length)
     images = jnp.sum((image_counts[0] > 0).astype(jnp.int32))
     member = (group_of_device[0] == lax.iota(jnp.int32, NGROUPS)).astype(jnp.int32)
-    totals = lax.psum(member * images, ("grp", "dp"))
+    totals = member * images
+    for position in range((lax.axis_size("grp") * lax.axis_size("dp")).bit_length() - 1):
+        totals = totals + swap(totals, 1 << position)
     factor = jnp.sum(member * group_weight).astype(jnp.float32) / jnp.sum(member * totals).astype(
         jnp.float32
     )
@@ -97,30 +291,9 @@
         jnp.dot(normed_one_low, qkv_weight, preferred_element_type=jnp.float32)
         + qkv_bias.astype(jnp.float32)
     ).astype(jnp.bfloat16)
-    query_rows = projected[:, :D].reshape(length, HEADS, HEAD_DIM)
-    key_rows = projected[:, D : 2 * D].reshape(length, HEADS, HEAD_DIM)
-    value_rows = projected[:, 2 * D :].reshape(length, HEADS, HEAD_DIM)
-    block_rows = min(512, length)
-    offsets = list(range(0, length, block_rows))
-    context_parts = []
-    log_sums = []
-    for offset in offsets:
-        same_segment = segment[offset : offset + block_rows, None] == segment[None, :]
-        scores = score_block(query_rows[offset : offset + block_rows], key_rows, same_segment)
-        row_max = jnp.max(scores, axis=-1, keepdims=True)
-        exponent = jnp.exp(scores - row_max)
-        row_sum = jnp.sum(exponent, axis=-1, keepdims=True)
-        attn_probs = exponent / row_sum
-        log_sums.append(row_max + jnp.log(row_sum))
-        context_parts.append(
-            jnp.einsum(
-                "hqk,khd->qhd",
-                attn_probs.astype(jnp.bfloat16),
-                value_rows,
-                preferred_element_type=jnp.float32,
-            )
-        )
-    context = jnp.concatenate(context_parts, axis=0).reshape(length, D).astype(jnp.bfloat16)
+    seg_col, seg_row = segment[:, None], segment[None, :]
+    pad_start = jnp.sum(image_counts[0], keepdims=True)
+    context = attn_forward(projected, seg_col, seg_row, pad_start)
     middle = inputs + (
         jnp.dot(context, proj_weight, preferred_element_type=jnp.float32)
         + proj_bias.astype(jnp.float32)
@@ -155,52 +328,10 @@
     grad_branch = grad_middle.astype(jnp.bfloat16)
     proj_grad = contract_rows(context, grad_branch)
     proj_bias_grad = jnp.sum(grad_branch.astype(jnp.float32), axis=0)
-    grad_context = (
-        contract_cols(grad_branch, proj_weight)
-        .astype(jnp.bfloat16)
-        .reshape(length, HEADS, HEAD_DIM)
-    )
-    grad_keys = jnp.zeros((length, HEADS, HEAD_DIM), jnp.float32)
-    grad_values = jnp.zeros((length, HEADS, HEAD_DIM), jnp.float32)
-    query_grads = []
-    for piece_index, offset in enumerate(offsets):
-        query_part = query_rows[offset : offset + block_rows]
-        context_grad_part = grad_context[offset : offset + block_rows]
-        same_segment = segment[offset : offset + block_rows, None] == segment[None, :]
-        attn_probs = jnp.exp(
-            score_block(query_part, key_rows, same_segment) - log_sums[piece_index]
-        )
-        grad_probs = jnp.einsum(
-            "qhd,khd->hqk", context_grad_part, value_rows, preferred_element_type=jnp.float32
-        )
-        grad_scores = (
-            attn_probs * (grad_probs - jnp.sum(attn_probs * grad_probs, axis=-1, keepdims=True))
-        ).astype(jnp.bfloat16)
-        query_grads.append(
-            jnp.einsum("hqk,khd->qhd", grad_scores, key_rows, preferred_element_type=jnp.float32)
-            * 0.125
-        )
-        grad_keys = (
-            grad_keys
-            + jnp.einsum(
-                "hqk,qhd->khd", grad_scores, query_part, preferred_element_type=jnp.float32
-            )
-            * 0.125
-        )
-        grad_values = grad_values + jnp.einsum(
-            "hqk,qhd->khd",
-            attn_probs.astype(jnp.bfloat16),
-            context_grad_part,
-            preferred_element_type=jnp.float32,
-        )
+    grad_context = contract_cols(grad_branch, proj_weight).astype(jnp.bfloat16)
     grad_projected = jnp.concatenate(
-        [
-            jnp.concatenate(query_grads, axis=0).reshape(length, D),
-            grad_keys.reshape(length, D),
-            grad_values.reshape(length, D),
-        ],
-        axis=1,
-    ).astype(jnp.bfloat16)
+        attn_backward(projected, grad_context, seg_col, seg_row), axis=1
+    )
     qkv_grad = contract_rows(normed_one_low, grad_projected)
     qkv_bias_grad = jnp.sum(grad_projected.astype(jnp.float32), axis=0)
     grad_input_norm, gain_one_grad, shift_one_grad = norm_one_back(

time: 976 us -> 774 us (0.79)
  matrix products: 243 us -> 90 us
  other arithmetic: 222 us -> 161 us
  Pallas kernels: 0 us -> 55.7 us
  blocking collectives: 42.5 us -> 0 us
  local copies, waits for them, and re-layouts: 335 us -> 321 us
    dot_general x12 -> x0, matrix products: 151 us -> none  [the longest x2 39.7 us: on_device(): jnp.einsum('qhd,khd->hqk', context_grad_part, value_rows, preferred_eleme...]
    pallas_call x0 -> x2, Pallas kernels: none -> 55.7 us  [the longest x1 32.4 us: attn_backward(): pl.pallas_call(attn_backward_kernel, out_shape=[jax.ShapeDtypeStruct((len...]
    psum x1 -> x0, blocking collectives: 42.5 us -> none  [on_device(): totals = lax.psum(member * images, ('grp', 'dp'))]
    convert_element_type x1 -> x0, other arithmetic: 41.9 us -> none  [on_device(): grad_scores = (attn_probs * (grad_probs - jnp.sum(attn_probs * grad_probs...]
    reduce_sum x2 -> x1, other arithmetic: 25.8 us -> 1.29 us  [on_device(): pad_start = jnp.sum(image_counts[0], keepdims=True)]
    slice x8 -> x0, local copies, waits for them, and re-layouts: 12.7 us -> none  [the longest x3 6.42 us: on_device(): query_rows[offset:offset + block_rows]]
    unnamed x254 -> x175, local copies, waits for them, and re-layouts: 62.4 us -> 53.9 us
    ppermute x30 -> x35, starting transfers between devices: 28.1 us -> 34.8 us  [swap(): return lax.ppermute(values, AXES, [(i, i ^ bit) for i in range(count)])]
  transfers between devices with their start and end apart: 30 -> 35, of which waited for: 11 -> 16; matrix products, arithmetic and copies ran while one was open for 32% -> 60% of each run, Pallas kernels for 0% -> 7%
where the time goes in v2:
time: 774 us; the launch traced here: 760 us
  local copies, waits for them, and re-layouts  321 us (41%)
  other arithmetic  161 us (21%)
  waiting for transfers between devices  93.1 us (12%)
  matrix products  90 us (12%)
  Pallas kernels  55.7 us (7%)
  starting transfers between devices  34.8 us (4%)
    ppermute x35, waiting for transfers between devices, swap(): return lax.ppermute(values, AXES, [(i, i ^ bit) for i in range(count)])  93.1 us
    unnamed x175, local copies, waits for them, and re-layouts  53.9 us
    ppermute x35, starting transfers between devices, swap(): return lax.ppermute(values, AXES, [(i, i ^ bit) for i in range(count)])  34.8 us
    pallas_call x1, Pallas kernels, attn_backward(): pl.pallas_call(attn_backward_kernel, out_shape=[jax.ShapeDtypeStruct((len...  32.4 us
    dot_general x4, matrix products, contract_rows(): lax.dot_general(first_op, second_op, (((0,), (0,)), ((), ())), preferred_...  30.4 us
    dot_general x4, matrix products, contract_cols(): lax.dot_general(first_op, second_op, (((1,), (1,)), ((), ())), preferred_...  29.8 us
    concatenate x1, other arithmetic, on_device(): new_weights = jnp.concatenate(fresh, axis=1)  29.3 us
    concatenate x2, local copies, waits for them, and re-layouts, on_device(): jnp.concatenate([jnp.full((width,), flag, jnp.float32) for width, flag in...  26.2 us
  transfers between devices with their start and end apart: 35, of which 16 were waited for; matrix products, arithmetic and copies ran while one was open for 60% of the time, Pallas kernels for 7%

profile of v2, /device:TPU:0, one launch (start us, length us, event | category | flops | bytes accessed | tf_op | source)
XLA Modules:
  0.0 759.8 jit_solution(18071458183222127894)
XLA Ops:
  19.7 23.3 %attn_forward.1 = bf16[1024,768]{1,0:T(8,128)(2,1)S(1)} custom-call(s32[1]{0:T(128)} %bitcast.pad_ref, bf16[1024,2304]{1,0:T(8,128)(2,1)S(1)} %add_convert_fusion.query_ref.key_ref.value_ref, bf16[1024,2304]{1,0:T(8,128)(2,1)S(1)} %add_convert_fusion.query_ref.key_ref.value_ref, bf16[1024,2304]{1,0:T(8,128)(2,1)S(1)} %add_convert_fusion.query_ref.key_ref.value_ref, ...), custom_call_target="tpu_custom_call" | custom-call | flops 1207959552 | bytes 6291456 | tf_op jit(solution)/shard_map/attn_forward/pallas_call | solution.py:151
  50.0 11.3 %fusion.73 = f32[1024,3072]{1,0:T(8,128)} fusion(bf16[768,3072]{1,0:T(8,128)(2,1)} %param.32, f32[1024,768]{0,1:T(8,128)} %copy-done.4, f32[768]{0:T(1024)S(1)} %convert_element_type.287, f32[768]{0:T(1024)S(1)} %convert_element_type.286, f32[1024]{0:T(1024)S(1)} %fusion.58, f32[1024]{0:T(1024)S(1)} %broadcast_multiply_fusion), kind=kOutput, calls=%fused_computation.243 | convolution fusion | flops 4835770368 | bytes 20461568 | tf_op jit(solution)/shard_map/dot_general | solution.py:305
  61.3 16.1 %convert_reduce_fusion = (f32[3072]{0:T(1024)S(1)}, bf16[1024,3072]{1,0:T(8,128)(2,1)S(1)}) fusion(f32[1024,3072]{1,0:T(8,128)} %fusion.73, f32[3072]{0:T(1024)S(1)} %convert_element_type.289, bf16[3072,768]{1,0:T(8,128)(2,1)} %param.34, bf16[1024,768]{0,1:T(8,128)(2,1)S(1)} %copy-done.13, f32[1024]{0:T(1024)S(1)} %fusion.56), kind=kOutput, calls=%fused_computation.12 | convolution fusion | flops 4906546176 | bytes 25194496 | tf_op jit(solution)/shard_map/dot_general | solution.py:42
  99.4 32.4 %attn_backward.1 = (bf16[1024,768]{1,0:T(8,128)(2,1)S(1)}, bf16[1024,768]{1,0:T(8,128)(2,1)S(1)}, bf16[1024,768]{1,0:T(8,128)(2,1)S(1)}) custom-call(bf16[1024,2304]{1,0:T(8,128)(2,1)S(1)} %bitcast.269, bf16[1024,2304]{1,0:T(8,128)(2,1)S(1)} %bitcast.269, bf16[1024,2304]{1,0:T(8,128)(2,1)S(1)} %bitcast.269, ...), custom_call_target="tpu_custom_call" | custom-call | flops 3019898880 | bytes 11010048 | tf_op jit(solution)/shard_map/attn_backward/pallas_call | solution.py:223
  146.4 10.8 %fusion.29 = f32[3072,768]{1,0:T(8,128)} fusion(bf16[1024,768]{0,1:T(8,128)(2,1)S(1)} %copy-done.14, f32[1024]{0:T(1024)S(1)} %fusion.56, f32[1024,3072]{1,0:T(8,128)S(1)} %bitcast.283, f32[3072]{0:T(1024)S(1)} %convert_element_type.289), kind=kOutput, calls=%fused_computation.78 | convolution fusion | flops 4865654784 | bytes 23609344 | tf_op jit(solution)/shard_map/dot_general | solution.py:36
  168.6 12.0 %reshape.831 = f32[16,48,3,768]{3,2,1,0:T(4,128)} reshape(f32[768,2304]{1,0:T(8,128)} %fusion.69) | data formatting | bytes 14155776 | tf_op jit(solution)/shard_map/reshape | solution.py:532
  180.6 14.3 %fusion.78 = (f32[16,48,1,768]{3,2,1,0:T(1,128)}, f32[16,48,1,768]{3,2,1,0:T(1,128)S(1)}, f32[16,48,1,768]{3,2,1,0:T(1,128)}) fusion(f32[16,48,3,768]{3,2,1,0:T(4,128)} %reshape.831), kind=kLoop, calls=%fused_computation.245 | loop fusion | bytes 14155776 | tf_op jit(solution)/shard_map/slice | solution.py:533
  234.8 10.5 %fusion.72 = f32[768,3072]{1,0:T(8,128)} fusion(bf16[1024,3072]{1,0:T(8,128)(2,1)} %copy-done.70, f32[1024,768]{0,1:T(8,128)S(1)} %copy-done.6, f32[768]{0:T(1024)S(1)} %convert_element_type.287, f32[768]{0:T(1024)S(1)} %convert_element_type.286, f32[1024]{0:T(1024)S(1)} %fusion.58, f32[1024]{0:T(1024)S(1)} %broadcast_multiply_fusion), kind=kOutput, calls=%fused_computation.242 | convolution fusion | flops 4835770368 | bytes 18888704 | tf_op jit(solution)/shard_map/dot_general | solution.py:36
  245.3 12.4 %reshape.844 = f32[16,48,4,768]{3,2,1,0:T(4,128)} reshape(f32[768,3072]{1,0:T(8,128)} %fusion.72) | data formatting | bytes 18874368 | tf_op jit(solution)/shard_map/reshape | solution.py:511
  286.3 11.4 %collective-permute-done.8 = bf16[2,2,2,52,768]{4,1,0,3,2:T(2,128)(2,1)} collective-permute-done((bf16[2,2,2,52,768]{4,1,0,3,2:T(2,128)(2,1)}, bf16[2,2,2,52,768]{4,1,0,3,2:T(2,128)(2,1)}, u32[]{:S(2)}, u32[]{:S(2)}) %collective-permute-start.8) | collective-permute-done | bytes 639008 | tf_op jit(solution)/shard_map/ppermute | solution.py:426
  306.5 12.8 %multiply_reduce_fusion.3 = (f32[295152]{0:T(1024)}, f32[295152]{0:T(1024)}) fusion(f32[1,442992]{1,0:T(1,128)S(1)} %copy-done.42, f32[1,442992]{1,0:T(1,128)S(1)} %copy-done.43), kind=kLoop, calls=%fused_computation.101 | loop fusion | flops 590304 | bytes 4722432 | tf_op jit(solution)/shard_map/mul | solution.py:399
  372.4 14.0 %concatenate.213 = f32[295152]{0:T(1024)} concatenate(f32[147456]{0:T(1024)} %broadcast.223, f32[192]{0:T(256)} %broadcast_in_dim.95, f32[147456]{0:T(1024)} %broadcast.223, f32[48]{0:T(128)} %broadcast.222), dimensions={0} | concatenate | bytes 2361216 | tf_op jit(solution)/shard_map/concatenate | solution.py:391
  389.0 12.2 %concatenate.210 = f32[147840]{0:T(1024)} concatenate(f32[96]{0:T(128)} %broadcast.221, f32[110592]{0:T(1024)} %broadcast_in_dim.92, f32[144]{0:T(256)} %broadcast_in_dim.93, f32[36864]{0:T(1024)} %broadcast_in_dim.94, f32[48]{0:T(128)} %broadcast.222, f32[96]{0:T(128)} %broadcast.221), dimensions={0} | concatenate | bytes 1182720 | tf_op jit(solution)/shard_map/concatenate | solution.py:391
  406.6 13.7 %concatenate.208 = bf16[147840]{0:T(1024)(128)(2,1)} concatenate(bf16[48]{0:T(256)(128)(2,1)} %get-tuple-element.121, bf16[48]{0:T(256)(128)(2,1)} %get-tuple-element.122, bf16[110592]{0:T(1024)(128)(2,1)} %dynamic-slice_reduce_fusion.2, bf16[144]{0:T(256)(128)(2,1)} %fusion.59, bf16[36864]{0:T(1024)(128)(2,1)S(1)} %dynamic-slice_reduce_fusion.3, ...), dimensions={0} | concatenate | bytes 591360 | tf_op jit(solution)/shard_map/concatenate | solution.py:390
  427.2 8.3 %multiply_reduce_fusion.5 = (f32[147840]{0:T(1024)}, f32[147840]{0:T(1024)}) fusion(f32[1,442992]{1,0:T(1,128)} %param.37, f32[1,442992]{1,0:T(1,128)} %param.36), kind=kLoop, calls=%fused_computation.144 | loop fusion | flops 295680 | bytes 2365440 | tf_op jit(solution)/shard_map/mul | solution.py:399
  447.4 10.2 %concatenate.209 = f32[147840]{0:T(1024)} concatenate(f32[48]{0:T(128)S(1)} %get-tuple-element.92, f32[48]{0:T(128)S(1)} %get-tuple-element.91, f32[110592]{0:T(1024)} %reshape.843, f32[144]{0:T(256)S(1)} %bitcast.320, f32[36864]{0:T(1024)S(1)} %reshape_squeeze.9, f32[48]{0:T(128)S(1)} %get-tuple-element.90, f32[48]{0:T(128)S(1)} %get-tuple-element.89, f32[48]{0:T(128)S(1)} %get-tuple-element.88), dimensions={0} | concatenate | bytes 1182720 | tf_op jit(solution)/shard_map/concatenate | solution.py:389
  464.5 14.5 %collective-permute-done.19 = bf16[192,768]{1,0:T(8,128)(2,1)S(1)} collective-permute-done((bf16[192,768]{1,0:T(8,128)(2,1)S(1)}, bf16[192,768]{1,0:T(8,128)(2,1)S(1)}, u32[]{:S(2)}, u32[]{:S(2)}) %collective-permute-start.19) | collective-permute-done | bytes 294944 | tf_op jit(solution)/shard_map/ppermute | solution.py:426
  481.8 8.8 %dynamic-slice_reduce_fusion = (bf16[147456]{0:T(1024)(128)(2,1)}, bf16[147456]{0:T(1024)(128)(2,1)}) fusion(bf16[16,147456]{1,0:T(8,128)(2,1)} %reshape.860, s32[]{:T(128)S(6)} %select_n.324, bf16[16,147456]{1,0:T(8,128)(2,1)} %reshape.858), kind=kLoop, calls=%fused_computation.151 | loop fusion | bytes 1179652 | tf_op jit(solution)/shard_map/dynamic_slice | solution.py:364
  490.6 11.9 %concatenate.211 = bf16[295152]{0:T(1024)(128)(2,1)} concatenate(bf16[147456]{0:T(1024)(128)(2,1)} %get-tuple-element.120, bf16[192]{0:T(256)(128)(2,1)S(1)} %fusion.60, bf16[147456]{0:T(1024)(128)(2,1)} %get-tuple-element.119, bf16[48]{0:T(256)(128)(2,1)S(1)} %copy-done.68), dimensions={0} | concatenate | bytes 1180608 | tf_op jit(solution)/shard_map/concatenate | solution.py:390
  514.3 12.7 %concatenate.212 = f32[295152]{0:T(1024)} concatenate(f32[147456]{0:T(1024)} %reshape.847, f32[192]{0:T(256)S(1)} %bitcast.318, f32[147456]{0:T(1024)} %reshape_squeeze.11, f32[48]{0:T(128)S(1)} %get-tuple-element.87), dimensions={0} | concatenate | bytes 2361216 | tf_op jit(solution)/shard_map/concatenate | solution.py:389
  536.3 11.5 %collective-permute-done.28 = bf16[2,584,128]{2,1,0:T(8,128)(2,1)S(1)} collective-permute-done((bf16[2,584,128]{2,1,0:T(8,128)(2,1)S(1)}, bf16[2,584,128]{2,1,0:T(8,128)(2,1)S(1)}, u32[]{:S(2)}, u32[]{:S(2)}) %collective-permute-start.28) | collective-permute-done | bytes 299040 | tf_op jit(solution)/shard_map/ppermute | solution.py:426
  548.8 10.4 %add_convert_fusion.2 = bf16[1024,768]{0,1:T(8,128)(2,1)} fusion(f32[1024,768]{0,1:T(8,128)S(1)} %copy-done.6, bf16[3072,768]{1,0:T(8,128)(2,1)S(1)} %bitcast.293, f32[768]{0:T(1024)S(1)} %copy-done.67, f32[1024,3072]{1,0:T(8,128)} %fusion.73, f32[3072]{0:T(1024)S(1)} %copy-done.57), kind=kOutput, calls=%fused_computation.56 | convolution fusion | flops 4865654784 | bytes 22035456 | tf_op jit(solution)/shard_map/dot_general | solution.py:313
  584.1 9.6 %collective-permute-done.32 = bf16[2,2,584,128]{3,2,1,0:T(8,128)(2,1)S(1)} collective-permute-done((bf16[2,2,584,128]{3,2,1,0:T(8,128)(2,1)S(1)}, bf16[2,2,584,128]{3,2,1,0:T(8,128)(2,1)S(1)}, u32[]{:S(2)}, u32[]{:S(2)}) %collective-permute-start.32) | collective-permute-done | bytes 598048 | tf_op jit(solution)/shard_map/ppermute | solution.py:426
  598.1 21.7 %collective-permute-done.33 = bf16[2,2,2,584,128]{4,3,2,1,0:T(8,128)(2,1)S(1)} collective-permute-done((bf16[2,2,2,584,128]{4,3,2,1,0:T(8,128)(2,1)S(1)}, bf16[2,2,2,584,128]{4,3,2,1,0:T(8,128)(2,1)S(1)}, u32[]{:S(2)}, u32[]{:S(2)}) %collective-permute-start.33) | collective-permute-done | bytes 1196064 | tf_op jit(solution)/shard_map/ppermute | solution.py:426
  626.2 20.7 %concatenate.207 = f32[442992]{0:T(1024)} concatenate(f32[48]{0:T(128)S(1)} %get-tuple-element.92, f32[48]{0:T(128)S(1)} %get-tuple-element.91, f32[110592]{0:T(1024)S(1)} %copy-done.27, f32[144]{0:T(256)S(1)} %bitcast.321, f32[36864]{0:T(1024)} %copy-done.44, f32[48]{0:T(128)S(1)} %get-tuple-element.90, f32[48]{0:T(128)S(1)} %get-tuple-element.89, f32[48]{0:T(128)S(1)} %get-tuple-element.88, ...), dimensions={0} | concatenate | bytes 3543936 | tf_op jit(solution)/shard_map/concatenate | solution.py:413
  646.9 8.4 %broadcast_in_dim.91 = f32[1,442992]{1,0:T(1,128)} reshape(f32[442992]{0:T(1024)} %concatenate.207) | data formatting | bytes 3543936 | tf_op jit(solution)/shard_map/broadcast_in_dim | solution.py:413
  655.3 9.0 %broadcast_in_dim.96 = f32[1,442992]{1,0:T(1,128)} reshape(f32[442992]{0:T(1024)S(1)} %copy-done.18) | data formatting | bytes 3543936 | tf_op jit(solution)/shard_map/broadcast_in_dim | solution.py:414
  664.3 9.3 %broadcast_in_dim.97 = f32[1,442992]{1,0:T(1,128)} reshape(f32[442992]{0:T(1024)S(1)} %copy-done.19) | data formatting | bytes 3543936 | tf_op jit(solution)/shard_map/broadcast_in_dim | solution.py:415
  676.9 13.1 %copy.233 = bf16[2,8,1184,128]{3,1,2,0:T(8,128)(2,1)S(1)} copy(bf16[2,8,1184,128]{3,2,1,0:T(8,128)(2,1)S(1)} %bitcast.276) | data formatting | bytes 9699328
  692.3 11.6 %maximum_select_fusion = bf16[16,2,2,584,128]{4,3,2,0,1:T(8,128)(2,1)} fusion(bf16[16,1,2,584,128]{4,3,2,0,1:T(8,128)(2,1)} %bitcast.115, bf16[16,1,2,584,128]{4,3,2,0,1:T(8,128)(2,1)} %bitcast.113, pred[]{:T(512)S(6)} %eq.14), kind=kLoop, calls=%fused_computation.17 | loop fusion | flops 14352384 | bytes 19136512 | tf_op jit(solution)/shard_map/jit(_where)/select_n | solution.py:500
  712.0 17.3 %copy.232 = bf16[2,8,2336,128]{3,1,2,0:T(8,128)(2,1)S(1)} copy(bf16[2,8,2336,128]{3,2,1,0:T(8,128)(2,1)} %bitcast.273) | data formatting | bytes 19136512
  730.0 29.3 %pad_maximum_fusion = bf16[16,442992]{1,0:T(8,128)(2,1)} fusion(bf16[16,295152]{1,0:T(8,128)(2,1)S(1)} %slice.195, bf16[16,147840]{1,0:T(8,128)(2,1)S(1)} %bitcast.279), kind=kLoop, calls=%fused_computation.4 | loop fusion | flops 28351488 | bytes 28351488 | tf_op jit(solution)/shard_map/concatenate | solution.py:416
  (429 shorter events, 310.1 us)
Async XLA Ops:
  3.3 206.2 %collective-permute-start = (s32[3]{0:T(128)S(1)}, s32[3]{0:T(128)S(1)}, u32[]{:S(2)}, u32[]{:S(2)}) collective-permute-start(s32[3]{0:T(128)S(1)} %fusion.68), channel_id=1, source_target_pairs={{0,1},{1,0},{2,3},{3,2},{4,5},{5,4},{6,7},{7,6},{8,9},{9,8},{10,11... | collective-permute-start | bytes 44 | tf_op jit(solution)/shard_map/ppermute | solution.py:426
  217.9 4.4 collective-permute-start.3
  233.6 40.3 %collective-permute-start.5 = (bf16[16,104,768]{2,1,0:T(8,128)(2,1)}, bf16[16,104,768]{2,1,0:T(8,128)(2,1)}, u32[]{:S(2)}, u32[]{:S(2)}) collective-permute-start(bf16[16,104,768]{2,1,0:T(8,128)(2,1)} %dynamic-slice_bitcast_fusion.1), channel_id=1, source_target_pairs={{0,16},{1,17},{2,18},{3,19},{4,20},{5,21},{6,22},{7,23},{8,24},{9,... | collective-permute-start | bytes 7667720 | tf_op jit(solution)/shard_map/ppermute | solution.py:426
  273.7 53.7 %collective-permute-start.13 = (bf16[16,192,768]{2,1,0:T(8,128)(2,1)}, bf16[16,192,768]{2,1,0:T(8,128)(2,1)}, u32[]{:S(2)}, u32[]{:S(2)}) collective-permute-start(bf16[16,192,768]{2,1,0:T(8,128)(2,1)} %dynamic-slice_bitcast_fusion), channel_id=1, source_target_pairs={{0,16},{1,17},{2,18},{3,19},{4,20},{5,21},{6,22},{7,23},{8,24},{9,... | collective-permute-start | bytes 14155784 | tf_op jit(solution)/shard_map/ppermute | solution.py:426
  280.8 16.9 %collective-permute-start.8 = (bf16[2,2,2,52,768]{4,1,0,3,2:T(2,128)(2,1)}, bf16[2,2,2,52,768]{4,1,0,3,2:T(2,128)(2,1)}, u32[]{:S(2)}, u32[]{:S(2)}) collective-permute-start(bf16[2,2,2,52,768]{4,1,0,3,2:T(2,128)(2,1)} %bitcast.258), channel_id=1, source_target_pairs={{0,2},{1,3},{2,0},{3,1},{4,6},{5,7},{6,4},{7,5},{8,10},{9,11},{10,... | collective-permute-start | bytes 1916936 | tf_op jit(solution)/shard_map/ppermute | solution.py:426
  284.4 16.4 %collective-permute-start.6 = (bf16[2,2,2,52,768]{4,2,1,0,3:T(2,128)(2,1)S(1)}, bf16[2,2,2,52,768]{4,2,1,0,3:T(2,128)(2,1)S(1)}, u32[]{:S(2)}, u32[]{:S(2)}) collective-permute-start(bf16[2,2,2,52,768]{4,2,1,0,3:T(2,128)(2,1)S(1)} %bitcast.312), channel_id=1, source_target_pairs={{0,1},{1,0},{2,3},{3,2},{4,5},{5,4},{6,7},{7,6},{8,9},{9,8},{10,11... | collective-permute-start | bytes 1916936 | tf_op jit(solution)/shard_map/ppermute | solution.py:426
  300.5 19.0 %collective-permute-start.9 = (bf16[2,2,52,768]{3,1,0,2:T(2,128)(2,1)}, bf16[2,2,52,768]{3,1,0,2:T(2,128)(2,1)}, u32[]{:S(2)}, u32[]{:S(2)}) collective-permute-start(bf16[2,2,52,768]{3,1,0,2:T(2,128)(2,1)} %dynamic-slice_bitcast_fusion.4), channel_id=1, source_target_pairs={{0,1},{1,0},{2,3},{3,2},{4,5},{5,4},{6,7},{7,6},{8,9},{9,8},{10,11... | collective-permute-start | bytes 958472 | tf_op jit(solution)/shard_map/ppermute | solution.py:426
  304.8 16.1 %collective-permute-start.7 = (bf16[2,2,52,768]{3,1,0,2:T(2,128)(2,1)}, bf16[2,2,52,768]{3,1,0,2:T(2,128)(2,1)S(1)}, u32[]{:S(2)}, u32[]{:S(2)}) collective-permute-start(bf16[2,2,52,768]{3,1,0,2:T(2,128)(2,1)} %bitcast.260), channel_id=1, source_target_pairs={{0,2},{1,3},{2,0},{3,1},{4,6},{5,7},{6,4},{7,5},{8,10},{9,11},{10,... | collective-permute-start | bytes 958472 | tf_op jit(solution)/shard_map/ppermute | solution.py:426
  325.9 20.5 %collective-permute-start.10 = (bf16[2,104,768]{2,0,1:T(2,128)(2,1)}, bf16[2,104,768]{2,0,1:T(2,128)(2,1)S(1)}, u32[]{:S(2)}, u32[]{:S(2)}) collective-permute-start(bf16[2,104,768]{2,0,1:T(2,128)(2,1)} %copy.163), channel_id=1, source_target_pairs={{0,4},{1,5},{2,6},{3,7},{4,0},{5,1},{6,2},{7,3},{8,12},{9,13},{10,... | collective-permute-start | bytes 958472 | tf_op jit(solution)/shard_map/ppermute | solution.py:426
  336.6 84.8 %collective-permute-start.14 = (bf16[2,2,2,96,768]{4,3,0,1,2:T(8,128)(2,1)}, bf16[2,2,2,96,768]{4,3,0,1,2:T(8,128)(2,1)}, u32[]{:S(2)}, u32[]{:S(2)}) collective-permute-start(bf16[2,2,2,96,768]{4,3,0,1,2:T(8,128)(2,1)} %bitcast.257), channel_id=1, source_target_pairs={{0,1},{1,0},{2,3},{3,2},{4,5},{5,4},{6,7},{7,6},{8,9},{9,8},{10,11... | collective-permute-start | bytes 3538952 | tf_op jit(solution)/shard_map/ppermute | solution.py:426
  345.9 79.0 %collective-permute-start.16 = (bf16[2,2,2,96,768]{4,3,0,1,2:T(8,128)(2,1)}, bf16[2,2,2,96,768]{4,3,0,1,2:T(8,128)(2,1)}, u32[]{:S(2)}, u32[]{:S(2)}) collective-permute-start(bf16[2,2,2,96,768]{4,3,0,1,2:T(8,128)(2,1)} %bitcast.256), channel_id=1, source_target_pairs={{0,2},{1,3},{2,0},{3,1},{4,6},{5,7},{6,4},{7,5},{8,10},{9,11},{10,... | collective-permute-start | bytes 3538952 | tf_op jit(solution)/shard_map/ppermute | solution.py:426
  348.2 72.1 %collective-permute-start.11 = (bf16[104,768]{1,0:T(8,128)(2,1)}, bf16[104,768]{1,0:T(8,128)(2,1)}, u32[]{:S(2)}, u32[]{:S(2)}) collective-permute-start(bf16[104,768]{1,0:T(8,128)(2,1)} %bitcast.262), channel_id=1, source_target_pairs={{0,8},{1,9},{2,10},{3,11},{4,12},{5,13},{6,14},{7,15},{8,0},{9,1},... | collective-permute-start | bytes 479240 | tf_op jit(solution)/shard_map/ppermute | solution.py:426
  421.3 14.2 %collective-permute-start.12 = (f32[104,768]{1,0:T(8,128)S(1)}, f32[104,768]{1,0:T(8,128)S(1)}, u32[]{:S(2)}, u32[]{:S(2)}) collective-permute-start(f32[104,768]{1,0:T(8,128)S(1)} %bitcast_add_fusion.3), channel_id=1, source_target_pairs={{0,16},{1,17},{2,18},{3,19},{4,20},{5,21},{6,22},{7,23},{8,24},{9,... | collective-permute-start | bytes 958472 | tf_op jit(solution)/shard_map/ppermute | solution.py:426
  423.3 15.8 %collective-permute-start.15 = (bf16[2,2,96,768]{3,2,0,1:T(8,128)(2,1)S(1)}, bf16[2,2,96,768]{3,2,0,1:T(8,128)(2,1)S(1)}, u32[]{:S(2)}, u32[]{:S(2)}) collective-permute-start(bf16[2,2,96,768]{3,2,0,1:T(8,128)(2,1)S(1)} %dynamic-slice_bitcast_fusion.3), channel_id=1, source_target_pairs={{0,2},{1,3},{2,0},{3,1},{4,6},{5,7},{6,4},{7,5},{8,10},{9,11},{10,... | collective-permute-start | bytes 1769480 | tf_op jit(solution)/shard_map/ppermute | solution.py:426
  426.6 15.5 %collective-permute-start.17 = (bf16[2,2,96,768]{3,2,0,1:T(8,128)(2,1)S(1)}, bf16[2,2,96,768]{3,2,0,1:T(8,128)(2,1)S(1)}, u32[]{:S(2)}, u32[]{:S(2)}) collective-permute-start(bf16[2,2,96,768]{3,2,0,1:T(8,128)(2,1)S(1)} %dynamic-slice_bitcast_fusion.2), channel_id=1, source_target_pairs={{0,1},{1,0},{2,3},{3,2},{4,5},{5,4},{6,7},{7,6},{8,9},{9,8},{10,11... | collective-permute-start | bytes 1769480 | tf_op jit(solution)/shard_map/ppermute | solution.py:426
  443.3 14.9 %collective-permute-start.18 = (bf16[2,192,768]{2,1,0:T(8,128)(2,1)}, bf16[2,192,768]{2,1,0:T(8,128)(2,1)}, u32[]{:S(2)}, u32[]{:S(2)}) collective-permute-start(bf16[2,192,768]{2,1,0:T(8,128)(2,1)} %fusion.52), channel_id=1, source_target_pairs={{0,4},{1,5},{2,6},{3,7},{4,0},{5,1},{6,2},{7,3},{8,12},{9,13},{10,... | collective-permute-start | bytes 1769480 | tf_op jit(solution)/shard_map/ppermute | solution.py:426
  459.9 19.1 %collective-permute-start.19 = (bf16[192,768]{1,0:T(8,128)(2,1)S(1)}, bf16[192,768]{1,0:T(8,128)(2,1)S(1)}, u32[]{:S(2)}, u32[]{:S(2)}) collective-permute-start(bf16[192,768]{1,0:T(8,128)(2,1)S(1)} %dynamic-slice_bitcast_fusion.5), channel_id=1, source_target_pairs={{0,8},{1,9},{2,10},{3,11},{4,12},{5,13},{6,14},{7,15},{8,0},{9,1},... | collective-permute-start | bytes 884744 | tf_op jit(solution)/shard_map/ppermute | solution.py:426
  461.8 19.3 %collective-permute-start.21 = (bf16[2,296,128]{2,1,0:T(8,128)(2,1)S(1)}, bf16[2,296,128]{2,1,0:T(8,128)(2,1)S(1)}, u32[]{:S(2)}, u32[]{:S(2)}) collective-permute-start(bf16[2,296,128]{2,1,0:T(8,128)(2,1)S(1)} %fusion.104), channel_id=1, source_target_pairs={{0,8},{1,9},{2,10},{3,11},{4,12},{5,13},{6,14},{7,15},{8,0},{9,1},... | collective-permute-start | bytes 454664 | tf_op jit(solution)/shard_map/ppermute | solution.py:426
  479.9 26.4 %collective-permute-start.20 = (f32[192,768]{1,0:T(8,128)}, f32[192,768]{1,0:T(8,128)}, u32[]{:S(2)}, u32[]{:S(2)}) collective-permute-start(f32[192,768]{1,0:T(8,128)} %convert_add_fusion.10), channel_id=1, source_target_pairs={{0,16},{1,17},{2,18},{3,19},{4,20},{5,21},{6,22},{7,23},{8,24},{9,... | collective-permute-start | bytes 1769480 | tf_op jit(solution)/shard_map/ppermute | solution.py:426
  481.8 22.5 %collective-permute-start.22 = (bf16[2,2,296,128]{3,2,1,0:T(8,128)(2,1)}, bf16[2,2,296,128]{3,2,1,0:T(8,128)(2,1)}, u32[]{:S(2)}, u32[]{:S(2)}) collective-permute-start(bf16[2,2,296,128]{3,2,1,0:T(8,128)(2,1)} %maximum_select_fusion.21), channel_id=1, source_target_pairs={{0,4},{1,5},{2,6},{3,7},{4,0},{5,1},{6,2},{7,3},{8,12},{9,13},{10,... | collective-permute-start | bytes 909320 | tf_op jit(solution)/shard_map/ppermute | solution.py:426
  532.1 15.7 %collective-permute-start.28 = (bf16[2,584,128]{2,1,0:T(8,128)(2,1)S(1)}, bf16[2,584,128]{2,1,0:T(8,128)(2,1)S(1)}, u32[]{:S(2)}, u32[]{:S(2)}) collective-permute-start(bf16[2,584,128]{2,1,0:T(8,128)(2,1)S(1)} %fusion.106), channel_id=1, source_target_pairs={{0,8},{1,9},{2,10},{3,11},{4,12},{5,13},{6,14},{7,15},{8,0},{9,1},... | collective-permute-start | bytes 897032 | tf_op jit(solution)/shard_map/ppermute | solution.py:426
  535.3 28.5 %collective-permute-start.25 = (bf16[2,2,296,128]{3,2,1,0:T(8,128)(2,1)}, bf16[2,2,296,128]{3,2,1,0:T(8,128)(2,1)}, u32[]{:S(2)}, u32[]{:S(2)}) collective-permute-start(bf16[2,2,296,128]{3,2,1,0:T(8,128)(2,1)} %get-tuple-element.103), channel_id=1, source_target_pairs={{0,1},{1,0},{2,3},{3,2},{4,5},{5,4},{6,7},{7,6},{8,9},{9,8},{10,11... | collective-permute-start | bytes 909320 | tf_op jit(solution)/shard_map/ppermute | solution.py:426
  535.8 29.7 %collective-permute-start.23 = (bf16[2,2,296,128]{3,2,1,0:T(8,128)(2,1)}, bf16[2,2,296,128]{3,2,1,0:T(8,128)(2,1)}, u32[]{:S(2)}, u32[]{:S(2)}) collective-permute-start(bf16[2,2,296,128]{3,2,1,0:T(8,128)(2,1)} %get-tuple-element.102), channel_id=1, source_target_pairs={{0,2},{1,3},{2,0},{3,1},{4,6},{5,7},{6,4},{7,5},{8,10},{9,11},{10,... | collective-permute-start | bytes 909320 | tf_op jit(solution)/shard_map/ppermute | solution.py:426
  548.8 18.7 %collective-permute-start.29 = (bf16[2,2,584,128]{3,2,1,0:T(8,128)(2,1)}, bf16[2,2,584,128]{3,2,1,0:T(8,128)(2,1)}, u32[]{:S(2)}, u32[]{:S(2)}) collective-permute-start(bf16[2,2,584,128]{3,2,1,0:T(8,128)(2,1)} %maximum_select_fusion.19), channel_id=1, source_target_pairs={{0,4},{1,5},{2,6},{3,7},{4,0},{5,1},{6,2},{7,3},{8,12},{9,13},{10,... | collective-permute-start | bytes 1794056 | tf_op jit(solution)/shard_map/ppermute | solution.py:426
  564.9 16.7 %collective-permute-start.26 = (bf16[2,2,2,296,128]{4,3,2,1,0:T(8,128)(2,1)S(1)}, bf16[2,2,2,296,128]{4,3,2,1,0:T(8,128)(2,1)S(1)}, u32[]{:S(2)}, u32[]{:S(2)}) collective-permute-start(bf16[2,2,2,296,128]{4,3,2,1,0:T(8,128)(2,1)S(1)} %maximum_select_fusion.17), channel_id=1, source_target_pairs={{0,2},{1,3},{2,0},{3,1},{4,6},{5,7},{6,4},{7,5},{8,10},{9,11},{10,... | collective-permute-start | bytes 1818632 | tf_op jit(solution)/shard_map/ppermute | solution.py:426
  566.7 16.7 %collective-permute-start.24 = (bf16[2,2,2,296,128]{4,3,2,1,0:T(8,128)(2,1)S(1)}, bf16[2,2,2,296,128]{4,3,2,1,0:T(8,128)(2,1)S(1)}, u32[]{:S(2)}, u32[]{:S(2)}) collective-permute-start(bf16[2,2,2,296,128]{4,3,2,1,0:T(8,128)(2,1)S(1)} %maximum_select_fusion.15), channel_id=1, source_target_pairs={{0,1},{1,0},{2,3},{3,2},{4,5},{5,4},{6,7},{7,6},{8,9},{9,8},{10,11... | collective-permute-start | bytes 1818632 | tf_op jit(solution)/shard_map/ppermute | solution.py:426
  569.5 24.2 %collective-permute-start.32 = (bf16[2,2,584,128]{3,2,1,0:T(8,128)(2,1)S(1)}, bf16[2,2,584,128]{3,2,1,0:T(8,128)(2,1)S(1)}, u32[]{:S(2)}, u32[]{:S(2)}) collective-permute-start(bf16[2,2,584,128]{3,2,1,0:T(8,128)(2,1)S(1)} %get-tuple-element.81), channel_id=1, source_target_pairs={{0,1},{1,0},{2,3},{3,2},{4,5},{5,4},{6,7},{7,6},{8,9},{9,8},{10,11... | collective-permute-start | bytes 1794056 | tf_op jit(solution)/shard_map/ppermute | solution.py:426
  573.4 22.1 %collective-permute-start.30 = (bf16[2,2,584,128]{3,2,1,0:T(8,128)(2,1)S(1)}, bf16[2,2,584,128]{3,2,1,0:T(8,128)(2,1)S(1)}, u32[]{:S(2)}, u32[]{:S(2)}) collective-permute-start(bf16[2,2,584,128]{3,2,1,0:T(8,128)(2,1)S(1)} %get-tuple-element.80), channel_id=1, source_target_pairs={{0,2},{1,3},{2,0},{3,1},{4,6},{5,7},{6,4},{7,5},{8,10},{9,11},{10,... | collective-permute-start | bytes 1794056 | tf_op jit(solution)/shard_map/ppermute | solution.py:426
  584.0 89.5 %collective-permute-start.27 = (bf16[16,2,296,128]{3,2,1,0:T(8,128)(2,1)S(1)}, bf16[16,2,296,128]{3,2,1,0:T(8,128)(2,1)}, u32[]{:S(2)}, u32[]{:S(2)}) collective-permute-start(bf16[16,2,296,128]{3,2,1,0:T(8,128)(2,1)S(1)} %bitcast.284), channel_id=1, source_target_pairs={{0,16},{1,17},{2,18},{3,19},{4,20},{5,21},{6,22},{7,23},{8,24},{9,... | collective-permute-start | bytes 7274504 | tf_op jit(solution)/shard_map/ppermute | solution.py:426
  593.9 25.9 %collective-permute-start.33 = (bf16[2,2,2,584,128]{4,3,2,1,0:T(8,128)(2,1)S(1)}, bf16[2,2,2,584,128]{4,3,2,1,0:T(8,128)(2,1)S(1)}, u32[]{:S(2)}, u32[]{:S(2)}) collective-permute-start(bf16[2,2,2,584,128]{4,3,2,1,0:T(8,128)(2,1)S(1)} %maximum_select_fusion.10), channel_id=1, source_target_pairs={{0,2},{1,3},{2,0},{3,1},{4,6},{5,7},{6,4},{7,5},{8,10},{9,11},{10,... | collective-permute-start | bytes 3588104 | tf_op jit(solution)/shard_map/ppermute | solution.py:426
  595.7 25.6 %collective-permute-start.31 = (bf16[2,2,2,584,128]{4,3,2,1,0:T(8,128)(2,1)S(1)}, bf16[2,2,2,584,128]{4,3,2,1,0:T(8,128)(2,1)S(1)}, u32[]{:S(2)}, u32[]{:S(2)}) collective-permute-start(bf16[2,2,2,584,128]{4,3,2,1,0:T(8,128)(2,1)S(1)} %maximum_select_fusion.8), channel_id=1, source_target_pairs={{0,1},{1,0},{2,3},{3,2},{4,5},{5,4},{6,7},{7,6},{8,9},{9,8},{10,11... | collective-permute-start | bytes 3588104 | tf_op jit(solution)/shard_map/ppermute | solution.py:426
  624.6 67.7 %collective-permute-start.34 = (bf16[16,2,584,128]{3,2,1,0:T(8,128)(2,1)}, bf16[16,2,584,128]{3,2,1,0:T(8,128)(2,1)}, u32[]{:S(2)}, u32[]{:S(2)}) collective-permute-start(bf16[16,2,584,128]{3,2,1,0:T(8,128)(2,1)} %bitcast.114), channel_id=1, source_target_pairs={{0,16},{1,17},{2,18},{3,19},{4,20},{5,21},{6,22},{7,23},{8,24},{9,... | collective-permute-start | bytes 14352392 | tf_op jit(solution)/shard_map/ppermute | solution.py:426
  (85 other events, 936.6 us)
